TPU v7x, 256 devices: a whole 4x4x8 slice. The times are simulated.
256 devices in a mesh: gossip: 32 (over y, z_hi, core), mp: 8 (over z_lo, x).
Axes of the slice: x: 4, y: 4, z: 8 (z_hi: 4, z_lo: 2; z = z_hi * 2 + z_lo), core: 2. Of those that a mesh axis runs over, the one named last changes fastest.
Arguments:
- params: float32 [32, 1024, 4096], P('gossip', None, 'mp'), may hold values from -6 to 6
- public: float32 [32, 1024, 64], P('gossip'), may hold values from -12 to 12
- gradients: bfloat16 [2, 32, 1024, 4096], P(None, 'gossip', None, 'mp'), may hold values from -130 to 130
- projection: float32 [4096, 64], P('mp'), may hold values from -0.09375 to 0.09375
- partners: int32 [2, 32], P(None, 'gossip'), may hold values from 0 to 31, as said below
Outputs:
- params_out: float32 [32, 1024, 4096], P('gossip', None, 'mp')
- public_out: float32 [32, 1024, 64], P('gossip')
- consensus: float32 [2], replicated
- grad_norm: float32 [2], replicated
Inputs may be any that keep to these rules, and one draw needn't show every extreme that they name: Each row is a pairing of the 32 replicas: partners[r, partners[r, i]] = i and partners[r, i] != i.
All inputs are finite; a program needn't handle non-finite values.
Results may differ from a plain program's by a relative error of at most 0.008.
Values may be sent and summed in bfloat16 or wider, within the bound.
No kernel may reach another device: no remote copies, remote signals or barrier semaphores. Data moves between devices by JAX's collectives and lax.ppermute only.
A program may use at most 64 MiB of HBM per device.

v0:
```python
import functools

import jax
import jax.numpy as jnp
from jax import lax
from jax.sharding import Mesh
from jax.sharding import PartitionSpec as P

ROUNDS = 2
GOSSIP = ("gossip_0", "gossip_1", "gossip_2")
MP = ("mp_0", "mp_1")
GOSSIP_MP = ("gossip_0", "gossip_1", "gossip_2", "mp_0", "mp_1")


step_size = 1.0
clip_limit = 0.5
mixing = 0.4
epsilon = 1e-06


def laid_out(pieces, dim):
    pieces = jnp.moveaxis(pieces, 0, dim)
    dims = pieces.shape
    return pieces.reshape(*dims[:dim], dims[dim] * dims[dim + 1], *dims[dim + 2 :])


def sent_to_all(x, axis):
    copies = jnp.broadcast_to(x, (lax.axis_size(axis), *x.shape))
    return lax.all_to_all(copies, axis, split_axis=0, concat_axis=0, tiled=True)


def collect(x, axis, dim):
    return laid_out(sent_to_all(x, axis), dim)


def by_axis(x, axes):
    return functools.reduce(lax.psum, axes, x)


def split_up(x, dim, size):
    dims = x.shape
    pieces = x.reshape(*dims[:dim], size, dims[dim] // size, *dims[dim + 1 :])
    return jnp.moveaxis(pieces, dim, 0)


def summed_on_arrival(x, axis, dim):
    size = lax.axis_size(axis)
    pieces = lax.all_to_all(split_up(x, dim, size), axis, 0, 0, tiled=True)
    return jnp.sum(pieces, axis=0)


def sent_together(arrays, axis, dim, along):
    widths = [a.shape[along] for a in arrays]
    both = jnp.concatenate(arrays, axis=along)
    whole = lax.all_gather(both, axis, axis=dim, tiled=True)
    return tuple(jnp.split(whole, [sum(widths[:k]) for k in range(1, len(widths))], axis=along))


def partner_rows(outgoing, table_row):
    initial = outgoing.shape
    entries = outgoing.size
    replicas = lax.axis_size(GOSSIP)
    pieces = outgoing.reshape(replicas, entries // replicas)
    spread = lax.all_to_all(pieces, GOSSIP, split_axis=0, concat_axis=0, tiled=True)
    reordered = jnp.take(spread, table_row, axis=0)
    back = lax.all_to_all(reordered, GOSSIP, split_axis=0, concat_axis=0, tiled=True)
    return back.reshape(initial)


def body(params, public, gradients, projection, partners):
    highest = lax.Precision.HIGHEST
    mp_count = lax.axis_size(MP)
    row_count = params.shape[1]
    total = lax.axis_size(GOSSIP) * row_count * projection.shape[0] * mp_count
    weights = params[0]
    public_state = public[0]
    drift_list = []
    norm_list = []
    whole_table = collect(partners, GOSSIP, 1)
    for round_index in range(ROUNDS):
        grad_local = gradients[round_index, 0].astype(jnp.float32)
        local_squares = jnp.sum(grad_local * grad_local)
        squares = by_axis(local_squares, GOSSIP_MP)
        norm_value = jnp.sqrt(squares / total + epsilon)
        norm_list.append(norm_value)
        scale = jnp.minimum(1.0, clip_limit / norm_value)
        half = weights - step_size * scale * grad_local
        table_row = whole_table[round_index]
        share = row_count // mp_count
        first_row = lax.axis_index(MP) * share
        coef_rows = public_state
        rebuilt = jnp.dot(coef_rows, projection.T, precision=highest)
        summed = summed_on_arrival(jnp.dot(half - rebuilt, projection, precision=highest), MP, 0)
        own_rows = lax.dynamic_slice_in_dim(public_state, first_row, share, 0)
        sent_share = (own_rows + summed).astype(jnp.bfloat16)
        mate_share = partner_rows(sent_share, table_row)
        sent, mate = sent_together((sent_share, mate_share), MP, 0, 1)
        public_state = sent.astype(jnp.float32)
        drift = jnp.dot(mate.astype(jnp.float32) - public_state, projection.T, precision=highest)
        weights = half + mixing * drift
        local_drift = jnp.sum(drift * drift)
        drift_list.append(by_axis(local_drift, GOSSIP_MP) / total)
    return (weights[None], public_state[None], jnp.stack(drift_list), jnp.stack(norm_list))


def solution(mesh):
    finer = Mesh(
        mesh.devices.reshape(4, 4, 2, 2, 4), ("gossip_0", "gossip_1", "gossip_2", "mp_0", "mp_1")
    )
    placed = (
        P(GOSSIP, None, MP),
        P(GOSSIP, None, None),
        P(None, GOSSIP, None, MP),
        P(MP, None),
        P(None, GOSSIP),
    )
    return jax.shard_map(
        body,
        mesh=finer,
        in_specs=placed,
        out_specs=(P(GOSSIP, None, MP), P(GOSSIP, None, None), P(), P()),
        check_vma=False,
    )
```

profile of v0, /device:TPU:1, one launch (start us, length us, event | category | flops | bytes accessed | tf_op | source)
XLA Modules:
  0.0 249.9 jit_solution(172169866287947021)
XLA Ops:
  2.0 12.8 %all-to-all-start.2 = ((s32[32,2,1]{1,2,0:T(1,128)}), s32[32,2,1]{1,2,0:T(1,128)S(1)}, u32[]{:S(2)}, u32[]{:S(2)}) async-start(s32[32,2,1]{1,2,0:T(1,128)} %broadcast_in_dim.18), calls=%async_computation.2 | async-start | bytes 32768 | tf_op jit(solution)/shard_map/all_to_all | solution.py:29
  17.6 9.2 %all-reduce.5 = (f32[]{:T(128)}, f32[]{:T(128)}) all-reduce(f32[]{:T(128)} %get-tuple-element.10, f32[]{:T(128)} %get-tuple-element.9), channel_id=1, replica_groups=mesh['gossip_0'=4,'gossip_1'=4,'gossip_2'=2,'mp_0'=2,'mp_1'=4] {'gossip_0'}, use_global_device_ids=true, to_apply=%region_1.0 | all-reduce | flops 2 | bytes 16 | tf_op jit(solution)/shard_map/psum | solution.py:37
  26.8 10.8 %all-reduce.3 = (f32[]{:T(128)}, f32[]{:T(128)}) all-reduce(f32[]{:T(128)} %get-tuple-element.23, f32[]{:T(128)} %get-tuple-element.24), channel_id=1, replica_groups=mesh['gossip_0'=4,'gossip_1'=4,'gossip_2'=2,'mp_0'=2,'mp_1'=4] {'gossip_1'}, use_global_device_ids=true, to_apply=%region_2.0 | all-reduce | flops 2 | bytes 16 | tf_op jit(solution)/shard_map/psum | solution.py:37
  37.7 7.1 %all-reduce.9 = (f32[]{:T(128)}, f32[]{:T(128)}) all-reduce(f32[]{:T(128)} %get-tuple-element.19, f32[]{:T(128)} %get-tuple-element.20), channel_id=1, replica_groups=mesh['gossip_0'=4,'gossip_1'=4,'gossip_2'=2,'mp_0'=2,'mp_1'=4] {'gossip_2'}, use_global_device_ids=true, to_apply=%region_3.0 | all-reduce | flops 2 | bytes 16 | tf_op jit(solution)/shard_map/psum | solution.py:37
  44.8 4.4 %all-reduce.7 = (f32[]{:T(128)}, f32[]{:T(128)}) all-reduce(f32[]{:T(128)} %get-tuple-element.31, f32[]{:T(128)} %get-tuple-element.32), channel_id=1, replica_groups=mesh['gossip_0'=4,'gossip_1'=4,'gossip_2'=2,'mp_0'=2,'mp_1'=4] {'mp_0'}, use_global_device_ids=true, to_apply=%region_4.0 | all-reduce | flops 2 | bytes 16 | tf_op jit(solution)/shard_map/psum | solution.py:37
  49.2 9.1 %all-reduce.1 = (f32[]{:T(128)}, f32[]{:T(128)}) all-reduce(f32[]{:T(128)} %get-tuple-element.27, f32[]{:T(128)} %get-tuple-element.28), channel_id=1, replica_groups=mesh['gossip_0'=4,'gossip_1'=4,'gossip_2'=2,'mp_0'=2,'mp_1'=4] {'mp_1'}, use_global_device_ids=true, to_apply=%region_5.0 | all-reduce | flops 2 | bytes 16 | tf_op jit(solution)/shard_map/psum | solution.py:37
  68.8 4.7 %all-to-all-done = f32[8,128,64]{1,2,0:T(8,128)S(1)} async-done(((f32[8,128,64]{1,2,0:T(8,128)}), f32[8,128,64]{1,2,0:T(8,128)S(1)}, u32[]{:S(2)}, u32[]{:S(2)}) %all-to-all-start) | async-done | bytes 262176 | tf_op jit(solution)/shard_map/all_to_all | solution.py:48
  75.7 8.7 %all-to-all-start.1 = ((bf16[32,2,128]{2,1,0:T(2,128)(2,1)}), bf16[32,2,128]{2,1,0:T(2,128)(2,1)S(1)}, u32[]{:S(2)}, u32[]{:S(2)}) async-start(bf16[32,2,128]{2,1,0:T(2,128)(2,1)} %reshape.105), calls=%async_computation.1 | async-start | bytes 32768 | tf_op jit(solution)/shard_map/all_to_all | solution.py:64
  84.5 9.3 %all-to-all-done.1 = bf16[32,2,128]{2,1,0:T(2,128)(2,1)S(1)} async-done(((bf16[32,2,128]{2,1,0:T(2,128)(2,1)}), bf16[32,2,128]{2,1,0:T(2,128)(2,1)S(1)}, u32[]{:S(2)}, u32[]{:S(2)}) %all-to-all-start.1) | async-done | bytes 16416 | tf_op jit(solution)/shard_map/all_to_all | solution.py:64
  95.7 4.1 %all-to-all-start.3 = ((bf16[32,2,128]{2,1,0:T(2,128)(2,1)}), bf16[32,2,128]{2,1,0:T(2,128)(2,1)S(1)}, u32[]{:S(2)}, u32[]{:S(2)}) async-start(bf16[32,2,128]{2,1,0:T(2,128)(2,1)} %reshape.107), calls=%async_computation.3 | async-start | bytes 32768 | tf_op jit(solution)/shard_map/all_to_all | solution.py:66
  100.6 8.7 %all-to-all-done.3 = bf16[32,2,128]{2,1,0:T(2,128)(2,1)S(1)} async-done(((bf16[32,2,128]{2,1,0:T(2,128)(2,1)}), bf16[32,2,128]{2,1,0:T(2,128)(2,1)S(1)}, u32[]{:S(2)}, u32[]{:S(2)}) %all-to-all-start.3) | async-done | bytes 16416 | tf_op jit(solution)/shard_map/all_to_all | solution.py:66
  109.6 20.0 %all_gather.6 = bf16[1024,128]{0,1:T(8,128)(2,1)S(1)} all-gather(bf16[128,128]{0,1:T(8,128)(2,1)S(1)} %pad_maximum_fusion), channel_id=1, replica_groups=mesh['gossip_0'=4,'gossip_1'=4,'gossip_2'=2,'mp_0'=2,'mp_1'=4] {'mp_0','..., dimensions={0}, use_global_device_ids=true | all-gather | bytes 294912 | tf_op jit(solution)/shard_map/all_gather | solution.py:55
  130.6 5.6 %multiply_reduce_fusion.1 = (f32[]{:T(128)}, f32[1024,512]{1,0:T(8,128)S(1)}) fusion(bf16[2,1,1024,512]{3,2,1,0:T(8,128)(2,1)} %param.9, f32[]{:T(128)S(6)} %min.7, f32[]{:T(128)S(6)} %min.6, f32[1,1024,512]{2,1,0:T(8,128)} %param.7, f32[512,64]{0,1:T(8,128)S(1)} %copy-done, bf16[1024,128]{0,1:T(8,128)(2,1)S(1)} %all_gather.6), kind=kOutput, calls=%fused_computation.13 | convolution fusion | flops 408092672 | bytes 6684684 | tf_op jit(solution)/shard_map/dot_general | solution.py:99
  142.6 6.0 %all-to-all-done.4 = f32[8,128,64]{1,2,0:T(8,128)S(1)} async-done(((f32[8,128,64]{1,2,0:T(8,128)}), f32[8,128,64]{1,2,0:T(8,128)S(1)}, u32[]{:S(2)}, u32[]{:S(2)}) %all-to-all-start.4) | async-done | bytes 262176 | tf_op jit(solution)/shard_map/all_to_all | solution.py:48
  150.2 9.7 %all-to-all-start.5 = ((bf16[32,2,128]{2,1,0:T(2,128)(2,1)}), bf16[32,2,128]{2,1,0:T(2,128)(2,1)S(1)}, u32[]{:S(2)}, u32[]{:S(2)}) async-start(bf16[32,2,128]{2,1,0:T(2,128)(2,1)} %reshape.109), calls=%async_computation.5 | async-start | bytes 32768 | tf_op jit(solution)/shard_map/all_to_all | solution.py:64
  159.9 9.4 %all-to-all-done.5 = bf16[32,2,128]{2,1,0:T(2,128)(2,1)S(1)} async-done(((bf16[32,2,128]{2,1,0:T(2,128)(2,1)}), bf16[32,2,128]{2,1,0:T(2,128)(2,1)S(1)}, u32[]{:S(2)}, u32[]{:S(2)}) %all-to-all-start.5) | async-done | bytes 16416 | tf_op jit(solution)/shard_map/all_to_all | solution.py:64
  171.3 4.1 %all-to-all-start.6 = ((bf16[32,2,128]{2,1,0:T(2,128)(2,1)}), bf16[32,2,128]{2,1,0:T(2,128)(2,1)S(1)}, u32[]{:S(2)}, u32[]{:S(2)}) async-start(bf16[32,2,128]{2,1,0:T(2,128)(2,1)} %reshape.111), calls=%async_computation.6 | async-start | bytes 32768 | tf_op jit(solution)/shard_map/all_to_all | solution.py:66
  176.0 8.8 %all-to-all-done.6 = bf16[32,2,128]{2,1,0:T(2,128)(2,1)S(1)} async-done(((bf16[32,2,128]{2,1,0:T(2,128)(2,1)}), bf16[32,2,128]{2,1,0:T(2,128)(2,1)S(1)}, u32[]{:S(2)}, u32[]{:S(2)}) %all-to-all-start.6) | async-done | bytes 16416 | tf_op jit(solution)/shard_map/all_to_all | solution.py:66
  185.1 19.8 %all_gather.7 = bf16[1024,128]{0,1:T(8,128)(2,1)S(1)} all-gather(bf16[128,128]{0,1:T(8,128)(2,1)S(1)} %pad_maximum_fusion.1), channel_id=1, replica_groups=mesh['gossip_0'=4,'gossip_1'=4,'gossip_2'=2,'mp_0'=2,'mp_1'=4] {'mp_0','..., dimensions={0}, use_global_device_ids=true | all-gather | bytes 294912 | tf_op jit(solution)/shard_map/all_gather | solution.py:55
  209.8 7.4 %all-reduce.4 = (f32[]{:T(128)}, f32[]{:T(128)}) all-reduce(f32[]{:T(128)} %get-tuple-element.37, f32[]{:T(128)} %get-tuple-element.35), channel_id=1, replica_groups=mesh['gossip_0'=4,'gossip_1'=4,'gossip_2'=2,'mp_0'=2,'mp_1'=4] {'gossip_0'}, use_global_device_ids=true, to_apply=%region_21.23 | all-reduce | flops 2 | bytes 16 | tf_op jit(solution)/shard_map/psum | solution.py:37
  217.2 8.2 %all-reduce.2 = (f32[]{:T(128)}, f32[]{:T(128)}) all-reduce(f32[]{:T(128)} %get-tuple-element.21, f32[]{:T(128)} %get-tuple-element.22), channel_id=1, replica_groups=mesh['gossip_0'=4,'gossip_1'=4,'gossip_2'=2,'mp_0'=2,'mp_1'=4] {'gossip_1'}, use_global_device_ids=true, to_apply=%region_22.24 | all-reduce | flops 2 | bytes 16 | tf_op jit(solution)/shard_map/psum | solution.py:37
  225.4 11.7 %all-reduce.8 = (f32[]{:T(128)}, f32[]{:T(128)}) all-reduce(f32[]{:T(128)} %get-tuple-element.17, f32[]{:T(128)} %get-tuple-element.18), channel_id=1, replica_groups=mesh['gossip_0'=4,'gossip_1'=4,'gossip_2'=2,'mp_0'=2,'mp_1'=4] {'gossip_2'}, use_global_device_ids=true, to_apply=%region_23.25 | all-reduce | flops 2 | bytes 16 | tf_op jit(solution)/shard_map/psum | solution.py:37
  237.0 4.5 %all-reduce.6 = (f32[]{:T(128)}, f32[]{:T(128)}) all-reduce(f32[]{:T(128)} %get-tuple-element.29, f32[]{:T(128)} %get-tuple-element.30), channel_id=1, replica_groups=mesh['gossip_0'=4,'gossip_1'=4,'gossip_2'=2,'mp_0'=2,'mp_1'=4] {'mp_0'}, use_global_device_ids=true, to_apply=%region_24.26 | all-reduce | flops 2 | bytes 16 | tf_op jit(solution)/shard_map/psum | solution.py:37
  241.5 6.6 %all-reduce = (f32[]{:T(128)}, f32[]{:T(128)}) all-reduce(f32[]{:T(128)} %get-tuple-element.25, f32[]{:T(128)} %get-tuple-element.26), channel_id=1, replica_groups=mesh['gossip_0'=4,'gossip_1'=4,'gossip_2'=2,'mp_0'=2,'mp_1'=4] {'mp_1'}, use_global_device_ids=true, to_apply=%region_25.27 | all-reduce | flops 2 | bytes 16 | tf_op jit(solution)/shard_map/psum | solution.py:37
  (68 shorter events, 35.6 us)
Async XLA Ops:
  0.6 58.4 %copy-start = (f32[512,64]{0,1:T(8,128)S(1)}, f32[512,64]{0,1:T(8,128)}, u32[]{:S(2)}) copy-start(f32[512,64]{0,1:T(8,128)} %param.10) | copy-start | bytes 393220
  0.6 58.4 %copy-start.3 = (f32[1,1024,64]{1,2,0:T(8,128)S(1)}, f32[1,1024,64]{1,2,0:T(8,128)}, u32[]{:S(2)}) copy-start(f32[1,1024,64]{1,2,0:T(8,128)} %param.8) | copy-start | bytes 786436
  2.0 62.1 %all-to-all-start.2 = ((s32[32,2,1]{1,2,0:T(1,128)}), s32[32,2,1]{1,2,0:T(1,128)S(1)}, u32[]{:S(2)}, u32[]{:S(2)}) async-start(s32[32,2,1]{1,2,0:T(1,128)} %broadcast_in_dim.18), calls=%async_computation.2 | async-start | bytes 32768 | tf_op jit(solution)/shard_map/all_to_all | solution.py:29
  14.7 46.2 %copy-start.1 = (bf16[2,1,1024,512]{3,2,1,0:T(8,128)(2,1)S(1)}, bf16[2,1,1024,512]{3,2,1,0:T(8,128)(2,1)}, u32[]{:S(2)}) copy-start(bf16[2,1,1024,512]{3,2,1,0:T(8,128)(2,1)} %param.9) | copy-start | bytes 6291460
  59.0 1.9 copy-start.2
  64.1 9.4 %all-to-all-start = ((f32[8,128,64]{1,2,0:T(8,128)}), f32[8,128,64]{1,2,0:T(8,128)S(1)}, u32[]{:S(2)}, u32[]{:S(2)}) async-start(f32[8,128,64]{1,2,0:T(8,128)} %bitcast.64), calls=%async_computation | async-start | bytes 524288 | tf_op jit(solution)/shard_map/all_to_all | solution.py:48
  75.7 18.0 %all-to-all-start.1 = ((bf16[32,2,128]{2,1,0:T(2,128)(2,1)}), bf16[32,2,128]{2,1,0:T(2,128)(2,1)S(1)}, u32[]{:S(2)}, u32[]{:S(2)}) async-start(bf16[32,2,128]{2,1,0:T(2,128)(2,1)} %reshape.105), calls=%async_computation.1 | async-start | bytes 32768 | tf_op jit(solution)/shard_map/all_to_all | solution.py:64
  95.7 13.5 %all-to-all-start.3 = ((bf16[32,2,128]{2,1,0:T(2,128)(2,1)}), bf16[32,2,128]{2,1,0:T(2,128)(2,1)S(1)}, u32[]{:S(2)}, u32[]{:S(2)}) async-start(bf16[32,2,128]{2,1,0:T(2,128)(2,1)} %reshape.107), calls=%async_computation.3 | async-start | bytes 32768 | tf_op jit(solution)/shard_map/all_to_all | solution.py:66
  139.1 9.4 %all-to-all-start.4 = ((f32[8,128,64]{1,2,0:T(8,128)}), f32[8,128,64]{1,2,0:T(8,128)S(1)}, u32[]{:S(2)}, u32[]{:S(2)}) async-start(f32[8,128,64]{1,2,0:T(8,128)} %bitcast.63), calls=%async_computation.4 | async-start | bytes 524288 | tf_op jit(solution)/shard_map/all_to_all | solution.py:48
  150.2 19.1 %all-to-all-start.5 = ((bf16[32,2,128]{2,1,0:T(2,128)(2,1)}), bf16[32,2,128]{2,1,0:T(2,128)(2,1)S(1)}, u32[]{:S(2)}, u32[]{:S(2)}) async-start(bf16[32,2,128]{2,1,0:T(2,128)(2,1)} %reshape.109), calls=%async_computation.5 | async-start | bytes 32768 | tf_op jit(solution)/shard_map/all_to_all | solution.py:64
  171.3 13.5 %all-to-all-start.6 = ((bf16[32,2,128]{2,1,0:T(2,128)(2,1)}), bf16[32,2,128]{2,1,0:T(2,128)(2,1)S(1)}, u32[]{:S(2)}, u32[]{:S(2)}) async-start(bf16[32,2,128]{2,1,0:T(2,128)(2,1)} %reshape.111), calls=%async_computation.6 | async-start | bytes 32768 | tf_op jit(solution)/shard_map/all_to_all | solution.py:66
where the time goes:
time: 253 us; the launch traced here: 250 us
  blocking collectives  119 us (47%)
  waiting for transfers between devices  46.7 us (18%)
  starting transfers between devices  46.3 us (18%)
  matrix products  17.1 us (7%)
  local copies, waits for them, and re-layouts  9.3 us (4%)
  other arithmetic  7.89 us (3%)
  between operations  3.64 us (1%)
    psum x10, blocking collectives, by_axis(): return functools.reduce(lax.psum, axes, x)  79 us
    all_gather x2, blocking collectives, sent_together(): whole = lax.all_gather(both, axis, axis=dim, tiled=True)  39.9 us
    all_to_all x2, waiting for transfers between devices, partner_rows(): lax.all_to_all(pieces, GOSSIP, split_axis=0, concat_axis=0, tiled=True)  18.6 us
    all_to_all x2, starting transfers between devices, partner_rows(): lax.all_to_all(pieces, GOSSIP, split_axis=0, concat_axis=0, tiled=True)  18.4 us
    all_to_all x2, waiting for transfers between devices, partner_rows(): lax.all_to_all(reordered, GOSSIP, split_axis=0, concat_axis=0, tiled=True)  17.5 us
    all_to_all x1, starting transfers between devices, sent_to_all(): return lax.all_to_all(copies, axis, split_axis=0, concat_axis=0, tiled=True)  12.8 us
    all_to_all x2, waiting for transfers between devices, summed_on_arrival(): pieces = lax.all_to_all(split_up(x, dim, size), axis, 0, 0, tiled=True)  10.6 us
    dot_general x2, matrix products, body(): jnp.dot(mate.astype(jnp.float32) - public_state, projection.T, precision=...  9.62 us
  transfers between devices with their start and end apart: 7, of which 6 were waited for; matrix products, arithmetic and copies ran while one was open for 4% of the time, Pallas kernels for 0%

commit v1 on v0

v1 whole, which is shorter than its diff:
```python
import functools

import jax
import jax.numpy as jnp
from jax import lax
from jax.experimental import pallas as pl
from jax.experimental.pallas import tpu as pltpu
from jax.sharding import PartitionSpec as P

F32 = jnp.float32
BF16 = jnp.bfloat16
AXES = ("gossip", "mp")
HIGHEST = lax.Precision.HIGHEST

NODES = 32
MP = 8
ROWS = 1024
RANK = 64
SLAB = 4096
DEVICES = 256
QUARTER = ROWS // 4
TOTAL = NODES * ROWS * SLAB

step_size = 1.0
clip_limit = 0.5
mixing = 0.4
epsilon = 1e-06


def lanes(shape):
    return lax.broadcasted_iota(jnp.int32, shape, 1)


def split_two(x):
    hi = x.astype(BF16)
    return hi, (x - hi.astype(F32)).astype(BF16)


def dot(a, b, **kw):
    return jnp.dot(a, b, preferred_element_type=F32, **kw)


def project_kernel(part_ref, w_ref, g_ref, c_ref, p_ref, out_ref, rhs, acc, stage, gram, squares, misc):
    k = pl.program_id(0)
    me = lax.axis_index("gossip")
    col = lax.axis_index("mp")

    @pl.when(k == 0)
    def _():
        p = p_ref[...]
        hi, lo = split_two(p)
        zero = jnp.zeros_like(hi)
        rhs[0] = jnp.concatenate([hi, zero, lo, zero], axis=1)
        rhs[1] = jnp.concatenate([zero, hi, zero, lo], axis=1)
        both = jnp.concatenate([p, p], axis=1)
        gram[...] = lax.dot_general(
            p, both, (((0,), (0,)), ((), ())), precision=HIGHEST, preferred_element_type=F32
        )
        squares[...] = jnp.zeros_like(squares)

    right = rhs[k % 2]
    w_hi, w_lo = split_two(w_ref[0])
    whole = dot(w_hi, right)
    values = [whole[:, :128] + whole[:, 128:] + dot(w_lo, right[:, :128])]
    for r in range(2):
        g = g_ref[r, 0]
        whole = dot(g, right)
        values.append(whole[:, :128] + whole[:, 128:])
        gf = g.astype(F32)
        squares[r] += jnp.sum((gf * gf).reshape(QUARTER // 8, 8, -1), axis=0)

    @pl.when(k % 2 == 0)
    def _():
        for a in range(3):
            acc[a] = values[a]

    for half in range(2):

        @pl.when(k == 2 * half + 1)
        def _():
            for a in range(3):
                stage[pl.ds(2 * a + half, QUARTER, 8), :] = acc[a] + values[a]

    @pl.when(k == col // 2)
    def _():
        c = c_ref[0]
        hi = c.astype(BF16).astype(F32)
        own = jnp.where(col % 2 == 0, hi, c - hi)
        misc[...] = jnp.concatenate([own, jnp.zeros_like(own)], axis=1)

    @pl.when(k == 3)
    def _():
        lane = lanes((1, 128))
        row = jnp.where(lane < RANK, gram[pl.ds(me, 1), :], gram[pl.ds(me + 32, 1), :])
        stage[pl.ds(6, QUARTER, 8), :] = jnp.broadcast_to(row, (QUARTER, 128))
        extra = jnp.zeros((1, 128), F32)
        for r in range(2):
            total = jnp.sum(squares[r], axis=(0, 1), keepdims=True)
            hi = total.astype(BF16).astype(F32)
            extra = jnp.where(lane == 64 + 2 * r, hi, extra)
            extra = jnp.where(lane == 65 + 2 * r, total - hi, extra)
            extra = jnp.where(lane == 68 + r, part_ref[r, 0].astype(F32), extra)
        stage[pl.ds(7, QUARTER, 8), :] = misc[...] + extra
        out_ref[...] = stage[...].reshape(DEVICES, 8, 128).astype(BF16)


def mix_kernel(in_ref, piece_ref, vec_ref, norm_ref, stage):
    stage[...] = in_ref[...].astype(F32).reshape(DEVICES * 8, 128)

    def loaded(m, j):
        return stage[pl.ds(8 * m + j, NODES, 8 * MP), :]

    def summed(j):
        return functools.reduce(lambda a, b: a + b, [loaded(m, j) for m in range(MP)])

    proj, back0, back1 = [
        jnp.concatenate([summed(2 * a), summed(2 * a + 1)], axis=1) for a in range(3)
    ]
    extras = [loaded(m, 7) for m in range(MP)]
    start = jnp.concatenate(
        [extras[2 * k][:, :RANK] + extras[2 * k + 1][:, :RANK] for k in range(4)], axis=1
    )
    lane = lanes((NODES, 128))
    every = functools.reduce(lambda a, b: a + b, extras)
    scales = []
    for r in range(2):
        chosen = (lane == 64 + 2 * r) | (lane == 65 + 2 * r)
        total = jnp.sum(jnp.where(chosen, every, 0.0), axis=(0, 1), keepdims=True)
        norm = jnp.sqrt(total / TOTAL + epsilon)
        scales.append(step_size * jnp.minimum(1.0, clip_limit / norm))
        norm_ref[r] = norm[0, 0]
    pairing = []
    for r in range(2):
        mate = jnp.sum(jnp.where(lane == 68 + r, extras[0], 0.0), axis=1, keepdims=True)
        column = lanes((NODES, NODES)).astype(F32)
        pairing.append(jnp.where(column == mate, 1.0, 0.0).astype(BF16))

    rows = summed(6)
    turned = pltpu.roll(rows, RANK, 1)
    twice = jnp.concatenate(
        [jnp.where(lane < RANK, rows, turned), jnp.where(lane < RANK, turned, rows)], axis=0
    )
    wide = jnp.concatenate([twice, twice], axis=1)
    tall = jnp.concatenate([wide] * 4, axis=0)
    square = (256, 256)
    same = lax.broadcasted_iota(jnp.int32, square, 0) // RANK == lanes(square) // RANK
    gram = jnp.where(same, tall, 0.0)

    def through(x):
        return dot(x, gram, precision=HIGHEST)

    stepped = proj - scales[0] * back0
    coef0 = start - through(start) + stepped
    sent0 = coef0.astype(BF16)
    own0 = sent0.astype(F32)
    drift0 = dot(pairing[0], sent0) - own0
    both = through(jnp.concatenate([drift0, own0], axis=0))
    moved0 = both[:NODES]
    coef1 = own0 - both[NODES:] + (stepped - scales[1] * back1) + mixing * moved0
    sent1 = coef1.astype(BF16)
    own1 = sent1.astype(F32)
    drift1 = dot(pairing[1], sent1) - own1
    moved1 = through(drift1)
    extra = jnp.zeros((NODES, 128), F32)
    for r, (d, moved) in enumerate(((drift0, moved0), (drift1, moved1))):
        total = jnp.sum(d * moved, axis=(0, 1), keepdims=True)
        hi = total.astype(BF16).astype(F32)
        extra = jnp.where(lane == 2 * r, hi, extra)
        extra = jnp.where(lane == 2 * r + 1, total - hi, extra)
    piece_ref[...] = jnp.concatenate(
        [drift0 + drift1, extra, own1, jnp.zeros((NODES, 128), F32)], axis=1
    ).astype(BF16)
    vec_ref[...] = jnp.concatenate(
        [jnp.broadcast_to(scales[0], (8, 128)), jnp.broadcast_to(scales[1], (8, 128))], axis=0
    )


def blend_kernel(in_ref, vec_ref, w_ref, g_ref, p_ref, out_ref, pub_ref, cons_ref, right):
    k = pl.program_id(0)

    @pl.when(k == 0)
    def _():
        hi, lo = split_two(p_ref[...].T)
        right[0] = jnp.concatenate([hi] * 4, axis=0)
        right[1] = jnp.concatenate([lo] * 4, axis=0)
        extra = in_ref[:, 256:384].astype(F32)
        lane = lanes((DEVICES, 128))
        for r in range(2):
            chosen = (lane == 2 * r) | (lane == 2 * r + 1)
            total = jnp.sum(jnp.where(chosen, extra, 0.0), axis=(0, 1), keepdims=True)
            cons_ref[r] = (total / TOTAL)[0, 0]

    square = (DEVICES, 256)
    mine = lanes(square) // RANK == k
    zero = jnp.zeros(square, BF16)
    moved = jnp.where(mine, in_ref[:, :256], zero)
    drift = dot(moved, right[0]) + dot(moved, right[1])
    scale0 = vec_ref[0:1, 0:1]
    scale1 = vec_ref[8:9, 0:1]
    half = w_ref[0] - scale0 * g_ref[0, 0].astype(F32) - scale1 * g_ref[1, 0].astype(F32)
    out_ref[0] = half + mixing * drift
    pick = (lax.broadcasted_iota(jnp.int32, (256, RANK), 0) % RANK == lanes((256, RANK))).astype(F32)
    sent = jnp.where(mine, in_ref[:, 384:640], zero)
    pub_ref[0] = dot(sent, pick.astype(BF16))


def body(params, public, gradients, projection, partners):
    width = params.shape[2]
    smem = pl.BlockSpec(memory_space=pltpu.SMEM)
    w_spec = pl.BlockSpec((1, QUARTER, width), lambda k: (0, k, 0))
    g_spec = pl.BlockSpec((2, 1, QUARTER, width), lambda k: (0, 0, k, 0))
    c_spec = pl.BlockSpec((1, QUARTER, RANK), lambda k: (0, k, 0))
    p_spec = pl.BlockSpec((width, RANK), lambda k: (0, 0))
    limit = pltpu.CompilerParams(vmem_limit_bytes=48 << 20)
    outgoing = pl.pallas_call(
        project_kernel,
        grid=(4,),
        out_shape=jax.ShapeDtypeStruct((DEVICES, 8, 128), BF16),
        in_specs=[smem, w_spec, g_spec, c_spec, p_spec],
        out_specs=pl.BlockSpec((DEVICES, 8, 128), lambda k: (0, 0, 0)),
        scratch_shapes=[
            pltpu.VMEM((2, width, 256), BF16),
            pltpu.VMEM((3, QUARTER, 128), F32),
            pltpu.VMEM((DEVICES * 8, 128), F32),
            pltpu.VMEM((RANK, 128), F32),
            pltpu.VMEM((2, 8, width), F32),
            pltpu.VMEM((QUARTER, 128), F32),
        ],
        compiler_params=limit,
    )(partners, params, gradients, public, projection)
    arrived = lax.all_to_all(outgoing, AXES, 0, 0, tiled=True)
    piece, scales, norms = pl.pallas_call(
        mix_kernel,
        out_shape=(
            jax.ShapeDtypeStruct((NODES, 768), BF16),
            jax.ShapeDtypeStruct((16, 128), F32),
            jax.ShapeDtypeStruct((2,), F32),
        ),
        out_specs=(
            pl.BlockSpec(memory_space=pltpu.VMEM),
            pl.BlockSpec(memory_space=pltpu.VMEM),
            smem,
        ),
        scratch_shapes=[pltpu.VMEM((DEVICES * 8, 128), F32)],
        compiler_params=limit,
    )(arrived)
    spread = jnp.broadcast_to(piece.reshape(NODES, 1, 2, 384), (NODES, MP, 2, 384))
    spread = spread.reshape(DEVICES, 2, 384)
    back = lax.all_to_all(spread, AXES, 0, 0, tiled=True).reshape(DEVICES, 768)
    weights, state, consensus = pl.pallas_call(
        blend_kernel,
        grid=(4,),
        out_shape=(
            jax.ShapeDtypeStruct(params.shape, F32),
            jax.ShapeDtypeStruct(public.shape, F32),
            jax.ShapeDtypeStruct((2,), F32),
        ),
        in_specs=[
            pl.BlockSpec((DEVICES, 768), lambda k: (0, 0)),
            pl.BlockSpec((16, 128), lambda k: (0, 0)),
            w_spec,
            g_spec,
            p_spec,
        ],
        out_specs=(w_spec, c_spec, smem),
        scratch_shapes=[pltpu.VMEM((2, 256, width), BF16)],
        compiler_params=limit,
    )(back, scales, params, gradients, projection)
    return weights, state, consensus, norms


def solution(mesh):
    placed = (
        P("gossip", None, "mp"),
        P("gossip", None, None),
        P(None, "gossip", None, "mp"),
        P("mp", None),
        P(None, "gossip"),
    )
    return jax.shard_map(
        body,
        mesh=mesh,
        in_specs=placed,
        out_specs=(P("gossip", None, "mp"), P("gossip", None, None), P(), P()),
        check_vma=False,
    )
```

time: 253 us -> 78.9 us (0.31); the launches traced: 250 us -> 78.6 us
  blocking collectives: 119 us -> 60.8 us
  waiting for transfers between devices: 46.7 us -> 0 us
  starting transfers between devices: 46.3 us -> 0 us
  matrix products: 17.1 us -> 0 us
  Pallas kernels: 0 us -> 8.19 us
  other arithmetic: 7.89 us -> 0 us
  between operations: 3.64 us -> 0.71 us
    psum x10 -> x0, blocking collectives: 79 us -> none  [by_axis(): return functools.reduce(lax.psum, axes, x)]
    all_to_all x0 -> x2, blocking collectives: none -> 60.8 us  [the longest x1 36.5 us: body(): arrived = lax.all_to_all(outgoing, AXES, 0, 0, tiled=True)]
    all_to_all x7 -> x0, waiting for transfers between devices: 46.7 us -> none  [the longest x2 18.6 us: partner_rows(): lax.all_to_all(pieces, GOSSIP, split_axis=0, concat_axis=0, tiled=True)]
    all_to_all x7 -> x0, starting transfers between devices: 46.3 us -> none  [the longest x2 18.4 us: partner_rows(): lax.all_to_all(pieces, GOSSIP, split_axis=0, concat_axis=0, tiled=True)]
    all_gather x2 -> x0, blocking collectives: 39.9 us -> none  [sent_together(): whole = lax.all_gather(both, axis, axis=dim, tiled=True)]
    dot_general x6 -> x0, matrix products: 17.1 us -> none  [the longest x2 9.62 us: body(): jnp.dot(mate.astype(jnp.float32) - public_state, projection.T, precision=...]
    pallas_call x0 -> x3, Pallas kernels: none -> 8.19 us  [the longest x1 3.47 us: body(): pl.pallas_call(project_kernel, grid=(4,), out_shape=jax.ShapeDtypeStruct(...]
    unnamed x18 -> x13, local copies, waits for them, and re-layouts: 2.56 us -> 8.62 us
  transfers between devices with their start and end apart: 7 -> 0, of which waited for: 6 -> 0; matrix products, arithmetic and copies ran while one was open for 4% -> 0% of each run, Pallas kernels for 0% -> 0%
where the time goes in v1:
time: 78.9 us; the launch traced here: 78.6 us
  blocking collectives  60.8 us (77%)
  local copies, waits for them, and re-layouts  8.85 us (11%)
  Pallas kernels  8.19 us (10%)
    all_to_all x1, blocking collectives, body(): arrived = lax.all_to_all(outgoing, AXES, 0, 0, tiled=True)  36.5 us
    all_to_all x1, blocking collectives, body(): back = lax.all_to_all(spread, AXES, 0, 0, tiled=True).reshape(DEVICES, 768)  24.3 us
    unnamed x13, local copies, waits for them, and re-layouts  8.62 us
    pallas_call x1, Pallas kernels, body(): pl.pallas_call(project_kernel, grid=(4,), out_shape=jax.ShapeDtypeStruct(...  3.47 us
    pallas_call x1, Pallas kernels, body(): pl.pallas_call(blend_kernel, grid=(4,), out_shape=(jax.ShapeDtypeStruct(p...  3.01 us
    pallas_call x1, Pallas kernels, body(): pl.pallas_call(mix_kernel, out_shape=(jax.ShapeDtypeStruct((NODES, 768),...  1.71 us

profile of v1, /device:TPU:1, one launch (start us, length us, event | category | flops | bytes accessed | tf_op | source)
XLA Modules:
  0.0 78.6 jit_solution(17359820992487264409)
XLA Ops:
  0.6 0.7 copy.9.part_ref
  1.4 1.0 %copy.11.p_ref = f32[512,64]{1,0:T(8,128)S(1)} copy(f32[512,64]{0,1:T(8,128)} %param.8) | data formatting | bytes 262144 | tf_op args[3]
  2.4 1.1 %copy.10.c_ref = f32[1,1024,64]{2,1,0:T(8,128)S(1)} copy(f32[1,1024,64]{1,2,0:T(8,128)} %param.6) | data formatting | bytes 524288 | tf_op args[1]
  3.6 0.0 copy-start
  3.6 1.6 %copy-done = f32[1,1024,512]{2,1,0:T(8,128)S(1)} copy-done((f32[1,1024,512]{2,1,0:T(8,128)S(1)}, f32[1,1024,512]{2,1,0:T(8,128)}, u32[]{:S(2)}) %copy-start) | copy-done | bytes 2097176
  5.2 0.0 copy-start.2
  5.2 1.6 %copy-done.2 = bf16[2,1,1024,512]{3,2,1,0:T(8,128)(2,1)S(1)} copy-done((bf16[2,1,1024,512]{3,2,1,0:T(8,128)(2,1)S(1)}, bf16[2,1,1024,512]{3,2,1,0:T(8,128)(2,1)}, u32[]{:S(2)}) %copy-start.2) | copy-done | bytes 2097176
  6.7 3.5 %shard_map.84 = bf16[256,8,128]{2,1,0:T(8,128)(2,1)S(1)} custom-call(s32[2,1]{1,0:T(2,128)S(1)} %copy.9.part_ref, f32[1,1024,512]{2,1,0:T(8,128)S(1)} %copy-done, bf16[2,1,1024,512]{3,2,1,0:T(8,128)(2,1)S(1)} %copy-done.2, f32[1,1024,64]{2,1,0:T(8,128)S(1)} %copy.10.c_ref, f32[512,64]{1,0:T(8,128)S(1)} %copy.11.p_ref), custom_call_target="tpu_custom_call" | custom-call | tf_op jit(solution)/shard_map/pallas_call | solution.py:215
  10.2 0.0 copy-start.1
  10.2 36.5 %all_to_all.10.in_ref = bf16[256,8,128]{2,1,0:T(8,128)(2,1)S(1)} all-to-all(bf16[256,8,128]{2,1,0:T(8,128)(2,1)S(1)} %shard_map.84), channel_id=1, replica_groups=mesh['gossip'=32,'mp'=8] {'gossip','mp'}, dimensions={0} | all-to-all | bytes 1048576 | tf_op jit(solution)/shard_map/all_to_all | solution.py:231
  46.8 1.7 %shard_map.85 = (bf16[32,768]{1,0:T(8,128)(2,1)S(1)}, f32[16,128]{1,0:T(8,128)S(1)}, f32[2]{0:T(128)}) custom-call(bf16[256,8,128]{2,1,0:T(8,128)(2,1)S(1)} %all_to_all.10.in_ref), custom_call_target="tpu_custom_call" | custom-call | tf_op jit(solution)/shard_map/pallas_call | solution.py:232
  48.5 0.2 broadcast_in_dim.8
  48.7 24.3 %all_to_all.11 = bf16[256,2,384]{2,1,0:T(2,128)(2,1)S(1)} all-to-all(bf16[256,2,384]{2,1,0:T(2,128)(2,1)S(1)} %bitcast.4), channel_id=1, replica_groups=mesh['gossip'=32,'mp'=8] {'gossip','mp'}, dimensions={0} | all-to-all | bytes 786432 | tf_op jit(solution)/shard_map/all_to_all | solution.py:249
  73.0 0.1 copy.14
  73.1 0.0 copy-done.1
  73.1 0.0 copy-start.3
  73.1 1.6 %copy-done.3 = bf16[2,1,1024,512]{3,2,1,0:T(8,128)(2,1)S(1)} copy-done((bf16[2,1,1024,512]{3,2,1,0:T(8,128)(2,1)S(1)}, bf16[2,1,1024,512]{3,2,1,0:T(8,128)(2,1)}, u32[]{:S(2)}) %copy-start.3) | copy-done | bytes 2097176
  74.7 3.0 %shard_map.86 = (f32[1,1024,512]{2,1,0:T(8,128)}, f32[1,1024,64]{2,1,0:T(8,128)S(1)}, f32[2]{0:T(128)}) custom-call(bf16[256,768]{1,0:T(8,128)(2,1)S(1)} %bitcast.3, f32[16,128]{1,0:T(8,128)S(1)} %get-tuple-element.11.vec_ref, f32[1,1024,512]{2,1,0:T(8,128)S(1)} %copy-done.1, bf16[2,1,1024,512]{3,2,1,0:T(8,128)(2,1)S(1)} %copy-done.3, f32[512,64]{1,0:T(8,128)S(1)} %copy.11.p_ref), custom_call_target="tpu_custom_call" | custom-call | tf_op jit(solution)/shard_map/pallas_call | solution.py:250
  77.7 0.9 %copy.13 = f32[1,1024,64]{1,2,0:T(8,128)} copy(f32[1,1024,64]{2,1,0:T(8,128)S(1)} %get-tuple-element.17) | data formatting | bytes 524288
  (1 shorter events, 0.0 us)
Async XLA Ops:
  3.6 1.6 %copy-start = (f32[1,1024,512]{2,1,0:T(8,128)S(1)}, f32[1,1024,512]{2,1,0:T(8,128)}, u32[]{:S(2)}) copy-start(f32[1,1024,512]{2,1,0:T(8,128)} %w_ref.3) | copy-start | bytes 6291460
  5.2 1.6 %copy-start.2 = (bf16[2,1,1024,512]{3,2,1,0:T(8,128)(2,1)S(1)}, bf16[2,1,1024,512]{3,2,1,0:T(8,128)(2,1)}, u32[]{:S(2)}) copy-start(bf16[2,1,1024,512]{3,2,1,0:T(8,128)(2,1)} %g_ref.3) | copy-start | bytes 6291460
  10.2 62.9 %copy-start.1 = (f32[1,1024,512]{2,1,0:T(8,128)S(1)}, f32[1,1024,512]{2,1,0:T(8,128)}, u32[]{:S(2)}) copy-start(f32[1,1024,512]{2,1,0:T(8,128)} %w_ref.3) | copy-start | bytes 6291460
  73.1 1.6 %copy-start.3 = (bf16[2,1,1024,512]{3,2,1,0:T(8,128)(2,1)S(1)}, bf16[2,1,1024,512]{3,2,1,0:T(8,128)(2,1)}, u32[]{:S(2)}) copy-start(bf16[2,1,1024,512]{3,2,1,0:T(8,128)(2,1)} %g_ref.3) | copy-start | bytes 6291460

commit v2 on v1

v2 whole, which is shorter than its diff:
```python
import functools

import jax
import jax.numpy as jnp
from jax import lax
from jax.experimental import pallas as pl
from jax.experimental.pallas import tpu as pltpu
from jax.sharding import Mesh
from jax.sharding import PartitionSpec as P

F32 = jnp.float32
BF16 = jnp.bfloat16
HIGHEST = lax.Precision.HIGHEST

NODES = 32
MP = 8
ROWS = 1024
RANK = 64
SLAB = 4096
DEVICES = NODES * MP
SHARE = ROWS // MP
CHUNKS = 4
CHUNK = ROWS // CHUNKS
FIRST = 208
PARTS = (("w", 0, 512), ("w", 512, 1024), ("g0", 0, 1024), ("g1", 0, 1024))
MP_ORDER = ("mp_1", "mp_0")
GOSSIP_ORDER = ("gossip_2", "gossip_0", "gossip_1")
BACK_ORDER = ("gossip_2", "mp_1", "mp_0", "gossip_0", "gossip_1")
PLANE = NODES // 2
TOTAL = NODES * ROWS * SLAB

step_size = 1.0
clip_limit = 0.5
mixing = 0.4
epsilon = 1e-06


def lanes(shape):
    return lax.broadcasted_iota(jnp.int32, shape, 1)


def rounded(x):
    return x.astype(BF16).astype(F32)


def split_two(x):
    hi = x.astype(BF16)
    return hi, (x - hi.astype(F32)).astype(BF16)


def dot(a, b, **kw):
    return jnp.dot(a, b, preferred_element_type=F32, **kw)


def project_kernel(w_hbm, g_hbm, c_hbm, p_hbm, out_ref, own_ref, w, g, c, p, gram, sems):
    me = lax.axis_index(GOSSIP_ORDER)
    first = pl.multiple_of(lax.axis_index(MP_ORDER) * SHARE, SHARE)
    p_copy = pltpu.make_async_copy(p_hbm, p, sems.at[len(PARTS)])
    p_copy.start()
    loads = []
    for i, (name, begin, end) in enumerate(PARTS):
        rows = pl.ds(begin, end - begin)
        if name == "w":
            copy = pltpu.make_async_copy(w_hbm.at[0, rows], w.at[rows], sems.at[i])
        else:
            r = int(name[1])
            copy = pltpu.make_async_copy(g_hbm.at[r, 0, rows], g.at[r, rows], sems.at[i])
        copy.start()
        loads.append(copy)
    c_copy = pltpu.make_async_copy(c_hbm.at[:, pl.ds(first, SHARE)], c, sems.at[len(PARTS) + 1])
    c_copy.start()
    p_copy.wait()
    low = lanes((64, 128)) < RANK
    pt = p[...]
    hi = rounded(pt)
    lo = rounded(pt - hi)
    right = jnp.concatenate([hi, hi, lo, lo], axis=0).T.astype(BF16)
    gram[...] = lax.dot_general(
        pt, jnp.concatenate([pt, pt], axis=0), (((1,), (1,)), ((), ())),
        precision=HIGHEST, preferred_element_type=F32,
    )
    lane = lanes((1, 128))
    row = jnp.where(lane < RANK, gram[pl.ds(me, 1), :], gram[pl.ds(me + NODES, 1), :])
    row_hi = rounded(row)
    scalars = jnp.zeros((1, 128), F32)
    for (name, begin, end), copy in zip(PARTS, loads):

        def store(a, value):
            for s in range((end - begin) // SHARE):
                at = s * SHARE
                packed = jnp.where(low, value[at : at + 64], value[at + 64 : at + 128])
                out_ref[begin // SHARE + s, 64 * a : 64 * a + 64, :] = packed.astype(BF16)

        copy.wait()
        if name == "w":
            w_hi, w_lo = split_two(w[begin:end, :])
            whole = dot(w_hi, right)
            store(0, whole[:, :128] + whole[:, 128:] + dot(w_lo, right[:, :128]))
        else:
            r = int(name[1])
            grad = g[r]
            whole = dot(grad, right)
            store(1 + r, whole[:, :128] + whole[:, 128:])
            gf = grad.astype(F32)
            squares = jnp.sum((gf * gf).reshape(ROWS // 8, 8, -1), axis=0)
            total = jnp.sum(squares, axis=(0, 1), keepdims=True)
            hi = rounded(total)
            scalars = jnp.where(lane == 2 * r, hi, scalars)
            scalars = jnp.where(lane == 2 * r + 1, total - hi, scalars)
    c_copy.wait()
    ct = c[...].T
    own_ref[...] = jnp.concatenate([ct[:64], ct[64:]], axis=1)
    at = lax.broadcasted_iota(jnp.int32, (16, 128), 0)
    extra = jnp.where(at == 0, row_hi, jnp.where(at == 1, row - row_hi, jnp.where(at == 2, scalars, 0.0)))
    extra = extra.astype(BF16)
    for m in range(MP):
        out_ref[m, 192:FIRST, :] = extra


def gather_kernel(part_ref, in_ref, own_ref, out_ref):
    value = in_ref[0].astype(F32)
    for m in range(1, MP):
        value += in_ref[m].astype(F32)

    def halves(x):
        return [x[:32], x[32:]]

    wide = (NODES, 128)
    row = value[192:193] + value[193:194]
    row_hi = rounded(row)
    lane = lanes((1, 128))
    pair = value[194:195]
    scalars = jnp.zeros((1, 128), F32)
    for r in range(2):
        chosen = (lane == 2 * r) | (lane == 2 * r + 1)
        total = jnp.sum(jnp.where(chosen, pair, 0.0), axis=1, keepdims=True)
        hi = rounded(total)
        scalars = jnp.where(lane == 2 * r, hi, scalars)
        scalars = jnp.where(lane == 2 * r + 1, total - hi, scalars)
        mate = part_ref[0, r]
        place = (mate % 2) * PLANE + mate // 2
        scalars = jnp.where(lane == 4 + r, place.astype(F32), scalars)
    upper = halves(value[:64]) + halves(value[64:128])
    upper += [jnp.broadcast_to(row_hi, wide), jnp.zeros(wide, F32)]
    lower = halves(value[128:192]) + halves(own_ref[...])
    lower += [jnp.broadcast_to(row - row_hi, wide), jnp.broadcast_to(scalars, wide)]
    out_ref[...] = jnp.stack(
        [jnp.concatenate(upper, axis=1), jnp.concatenate(lower, axis=1)], axis=1
    ).astype(BF16)


def mix_kernel(in_ref, piece_ref, vec_ref, norm_ref):
    value = in_ref[...].astype(F32)
    upper, lower = value[:, 0, :], value[:, 1, :]
    proj, back0 = upper[:, :256], upper[:, 256:512]
    back1, start = lower[:, :256], lower[:, 256:512]
    rows = upper[:, 512:640] + lower[:, 512:640]
    scalars = lower[:, 640:]
    lane = lanes((NODES, 128))
    scales = []
    for r in range(2):
        chosen = (lane == 2 * r) | (lane == 2 * r + 1)
        total = jnp.sum(jnp.where(chosen, scalars, 0.0), axis=(0, 1), keepdims=True)
        norm = jnp.sqrt(total / TOTAL + epsilon)
        scales.append(step_size * jnp.minimum(1.0, clip_limit / norm))
        norm_ref[r] = norm[0, 0]
    pairing = []
    for r in range(2):
        mate = jnp.sum(jnp.where(lane == 4 + r, scalars, 0.0), axis=1, keepdims=True)
        column = lanes((NODES, NODES)).astype(F32)
        pairing.append(jnp.where(column == mate, 1.0, 0.0).astype(BF16))

    turned = pltpu.roll(rows, RANK, 1)
    twice = jnp.concatenate(
        [jnp.where(lane < RANK, rows, turned), jnp.where(lane < RANK, turned, rows)], axis=0
    )
    wide = jnp.concatenate([twice, twice], axis=1)
    tall = jnp.concatenate([wide] * 4, axis=0)
    square = (256, 256)
    same = lax.broadcasted_iota(jnp.int32, square, 0) // RANK == lanes(square) // RANK
    gram = jnp.where(same, tall, 0.0)

    def through(x):
        return dot(x, gram, precision=HIGHEST)

    stepped = proj - scales[0] * back0
    coef0 = start - through(start) + stepped
    sent0 = coef0.astype(BF16)
    own0 = sent0.astype(F32)
    drift0 = dot(pairing[0], sent0) - own0
    both = through(jnp.concatenate([drift0, own0], axis=0))
    moved0 = both[:NODES]
    coef1 = own0 - both[NODES:] + (stepped - scales[1] * back1) + mixing * moved0
    sent1 = coef1.astype(BF16)
    own1 = sent1.astype(F32)
    drift1 = dot(pairing[1], sent1) - own1
    moved1 = through(drift1)
    extra = jnp.zeros((NODES, 128), F32)
    for r, (d, moved) in enumerate(((drift0, moved0), (drift1, moved1))):
        total = jnp.sum(d * moved, axis=(0, 1), keepdims=True)
        hi = rounded(total)
        extra = jnp.where(lane == 2 * r, hi, extra)
        extra = jnp.where(lane == 2 * r + 1, total - hi, extra)
    piece = jnp.stack(
        [
            jnp.concatenate([drift0 + drift1, extra], axis=1),
            jnp.concatenate([own1, jnp.zeros((NODES, 128), F32)], axis=1),
        ],
        axis=1,
    ).astype(BF16)
    for core in range(2):
        for m in range(MP):
            piece_ref[core, m] = piece[core * PLANE : (core + 1) * PLANE]
    vec_ref[...] = jnp.concatenate(
        [jnp.broadcast_to(scales[0], (8, 128)), jnp.broadcast_to(scales[1], (8, 128))], axis=0
    )


def step_kernel(vec_ref, w_ref, g_ref, p_ref, out_ref, right_ref):
    scale0 = vec_ref[0:1, 0:1]
    scale1 = vec_ref[8:9, 0:1]
    out_ref[...] = w_ref[0] - scale0 * g_ref[0, 0].astype(F32) - scale1 * g_ref[1, 0].astype(F32)

    @pl.when(pl.program_id(0) == 0)
    def _():
        hi, lo = split_two(p_ref[...])
        right_ref[0] = jnp.concatenate([hi] * 4, axis=0)
        right_ref[1] = jnp.concatenate([lo] * 4, axis=0)


def blend_kernel(in_ref, half_ref, right_ref, out_hbm, pub_ref, cons_ref, out, sems):
    square = (SHARE, 256)
    block = lax.broadcasted_iota(jnp.int32, square, 0) // NODES
    wanted = jnp.where(block == 1, 2, jnp.where(block == 2, 1, block))
    mine = lanes(square) // RANK == wanted
    zero = jnp.zeros(square, BF16)
    pick = (lax.broadcasted_iota(jnp.int32, (256, RANK), 0) % RANK == lanes((256, RANK))).astype(F32)
    pick = pick.astype(BF16)

    def spread(m, begin):
        rows = [
            in_ref[(core * MP + m) * PLANE : (core * MP + m + 1) * PLANE, begin : begin + 256]
            for core in range(2)
        ]
        return jnp.where(mine, jnp.concatenate(rows * 4, axis=0), zero)

    copies = []
    per = CHUNK // SHARE
    for k in range(CHUNKS):
        moved = jnp.concatenate([spread(k * per + s, 0) for s in range(per)], axis=0)
        drift = dot(moved, right_ref[0]) + dot(moved, right_ref[1])
        at = pl.ds(k * CHUNK, CHUNK)
        out[at, :] = half_ref[at, :] + mixing * drift
        copy = pltpu.make_async_copy(out.at[at], out_hbm.at[0, at], sems.at[k])
        copy.start()
        copies.append(copy)
    for k in range(CHUNKS):
        sent = jnp.concatenate([spread(k * per + s, 384) for s in range(per)], axis=0)
        pub_ref[0, :, k * CHUNK : (k + 1) * CHUNK] = lax.dot_general(
            pick, sent, (((0,), (1,)), ((), ())), preferred_element_type=F32
        )
    extra = in_ref[:, 256:384].astype(F32)
    lane = lanes((DEVICES, 128))
    for r in range(2):
        chosen = (lane == 2 * r) | (lane == 2 * r + 1)
        total = jnp.sum(jnp.where(chosen, extra, 0.0), axis=(0, 1), keepdims=True)
        cons_ref[r] = (total / TOTAL)[0, 0]
    for copy in copies:
        copy.wait()


def body(params, public, gradients, projection, partners):
    width = params.shape[2]
    smem = pl.BlockSpec(memory_space=pltpu.SMEM)
    vmem = pl.BlockSpec(memory_space=pltpu.VMEM)
    hbm = pl.BlockSpec(memory_space=pltpu.HBM)
    limit = pltpu.CompilerParams(vmem_limit_bytes=32 << 20)
    columns = projection.T
    stay = [pltpu.with_memory_space_constraint(x, pltpu.HBM) for x in (params, gradients, public[0].T, columns)]
    outgoing, own = pl.pallas_call(
        project_kernel,
        out_shape=(
            jax.ShapeDtypeStruct((MP, FIRST, 128), BF16),
            jax.ShapeDtypeStruct((64, 128), F32),
        ),
        in_specs=[hbm, hbm, hbm, hbm],
        out_specs=(vmem, vmem),
        scratch_shapes=[
            pltpu.VMEM((ROWS, width), F32),
            pltpu.VMEM((2, ROWS, width), BF16),
            pltpu.VMEM((RANK, SHARE), F32),
            pltpu.VMEM((RANK, width), F32),
            pltpu.VMEM((RANK, 128), F32),
            pltpu.SemaphoreType.DMA((len(PARTS) + 2,)),
        ],
        compiler_params=limit,
    )(*stay)
    arrived = lax.all_to_all(outgoing, MP_ORDER, 0, 0, tiled=True)
    outgoing = pl.pallas_call(
        gather_kernel,
        out_shape=jax.ShapeDtypeStruct((NODES, 2, 768), BF16),
        in_specs=[smem, vmem, vmem],
        out_specs=vmem,
        compiler_params=limit,
    )(partners.T, arrived, own)
    arrived = lax.all_to_all(outgoing, GOSSIP_ORDER, 0, 0, tiled=True)
    piece, scales, norms = pl.pallas_call(
        mix_kernel,
        out_shape=(
            jax.ShapeDtypeStruct((2, MP, PLANE, 2, 384), BF16),
            jax.ShapeDtypeStruct((16, 128), F32),
            jax.ShapeDtypeStruct((2,), F32),
        ),
        in_specs=[vmem],
        out_specs=(vmem, vmem, smem),
        compiler_params=limit,
    )(arrived)
    spread = piece.reshape(DEVICES, 2, 384)
    back = lax.all_to_all(spread, BACK_ORDER, 0, 0, tiled=True).reshape(DEVICES, 768)
    half, right = pl.pallas_call(
        step_kernel,
        grid=(CHUNKS,),
        out_shape=(
            jax.ShapeDtypeStruct((ROWS, width), F32),
            jax.ShapeDtypeStruct((2, 256, width), BF16),
        ),
        in_specs=[
            pl.BlockSpec((16, 128), lambda k: (0, 0)),
            pl.BlockSpec((1, CHUNK, width), lambda k: (0, k, 0)),
            pl.BlockSpec((2, 1, CHUNK, width), lambda k: (0, 0, k, 0)),
            pl.BlockSpec((RANK, width), lambda k: (0, 0)),
        ],
        out_specs=(
            pl.BlockSpec((CHUNK, width), lambda k: (k, 0)),
            pl.BlockSpec((2, 256, width), lambda k: (0, 0, 0)),
        ),
        compiler_params=limit,
        cost_estimate=pl.CostEstimate(flops=4 * ROWS * width, bytes_accessed=12 * ROWS * width, transcendentals=0),
    )(scales, params, gradients, columns)
    weights, state, consensus = pl.pallas_call(
        blend_kernel,
        out_shape=(
            jax.ShapeDtypeStruct(params.shape, F32),
            jax.ShapeDtypeStruct((1, RANK, ROWS), F32),
            jax.ShapeDtypeStruct((2,), F32),
        ),
        in_specs=[vmem, vmem, vmem],
        out_specs=(hbm, vmem, smem),
        scratch_shapes=[pltpu.VMEM((ROWS, width), F32), pltpu.SemaphoreType.DMA((CHUNKS,))],
        compiler_params=limit,
    )(back, half, right)
    return weights, jnp.swapaxes(state, 1, 2), consensus, norms


def solution(mesh):
    finer = Mesh(
        mesh.devices.reshape(4, 4, 2, 2, 4), ("gossip_0", "gossip_1", "gossip_2", "mp_0", "mp_1")
    )
    gossip = ("gossip_0", "gossip_1", "gossip_2")
    mp = ("mp_0", "mp_1")
    return jax.shard_map(
        body,
        mesh=finer,
        in_specs=(P(gossip, None, mp), P(gossip, None, None), P(None, gossip, None, mp), P(mp, None), P(None, gossip)),
        out_specs=(P(gossip, None, mp), P(gossip, None, None), P(), P()),
        check_vma=False,
    )
```

time: 78.9 us -> 72.2 us (0.915)
  blocking collectives: 60.8 us -> 36.4 us
  waiting for transfers between devices: 0 us -> 14 us
  starting transfers between devices: 0 us -> 5.64 us
  local copies, waits for them, and re-layouts: 8.85 us -> 4.55 us
  Pallas kernels: 8.19 us -> 10.7 us
    all_to_all x2, blocking collectives: 60.8 us -> 36.4 us  [the longest x1 22.1 us: body(): arrived = lax.all_to_all(outgoing, GOSSIP_ORDER, 0, 0, tiled=True)]
    all_to_all x0 -> x1, waiting for transfers between devices: none -> 14 us  [body(): lax.all_to_all(spread, BACK_ORDER, 0, 0, tiled=True).reshape(DEVICES, 768)]
    all_to_all x0 -> x1, starting transfers between devices: none -> 5.64 us  [body(): lax.all_to_all(spread, BACK_ORDER, 0, 0, tiled=True).reshape(DEVICES, 768)]
    unnamed x13, local copies, waits for them, and re-layouts: 8.62 us -> 4.55 us
    pallas_call x3 -> x5, Pallas kernels: 8.19 us -> 10.7 us  [the longest x1 4.17 us: body(): pl.pallas_call(project_kernel, out_shape=(jax.ShapeDtypeStruct((MP, FIRST...]
  transfers between devices with their start and end apart: 0 -> 1, of which waited for: 0 -> 1; matrix products, arithmetic and copies ran while one was open for 0% -> 0% of each run, Pallas kernels for 0% -> 2%
where the time goes in v2:
time: 72.2 us; the launch traced here: 71.9 us
  blocking collectives  36.4 us (50%)
  waiting for transfers between devices  14 us (19%)
  Pallas kernels  10.7 us (15%)
  starting transfers between devices  5.64 us (8%)
  local copies, waits for them, and re-layouts  4.55 us (6%)
  between operations  0.74 us (1%)
    all_to_all x1, blocking collectives, body(): arrived = lax.all_to_all(outgoing, GOSSIP_ORDER, 0, 0, tiled=True)  22.1 us
    all_to_all x1, blocking collectives, body(): arrived = lax.all_to_all(outgoing, MP_ORDER, 0, 0, tiled=True)  14.2 us
    all_to_all x1, waiting for transfers between devices, body(): lax.all_to_all(spread, BACK_ORDER, 0, 0, tiled=True).reshape(DEVICES, 768)  14 us
    all_to_all x1, starting transfers between devices, body(): lax.all_to_all(spread, BACK_ORDER, 0, 0, tiled=True).reshape(DEVICES, 768)  5.64 us
    unnamed x13, local copies, waits for them, and re-layouts  4.55 us
    pallas_call x1, Pallas kernels, body(): pl.pallas_call(project_kernel, out_shape=(jax.ShapeDtypeStruct((MP, FIRST...  4.17 us
    pallas_call x1, Pallas kernels, body(): pl.pallas_call(blend_kernel, out_shape=(jax.ShapeDtypeStruct(params.shape...  2.36 us
    pallas_call x1, Pallas kernels, body(): pl.pallas_call(mix_kernel, out_shape=(jax.ShapeDtypeStruct((2, MP, PLANE,...  2.28 us
  transfers between devices with their start and end apart: 1, of which 1 were waited for; matrix products, arithmetic and copies ran while one was open for 0% of the time, Pallas kernels for 2%

profile of v2, /device:TPU:1, one launch (start us, length us, event | category | flops | bytes accessed | tf_op | source)
XLA Modules:
  0.0 71.9 jit_solution(6610022037911187996)
XLA Ops:
  0.6 0.0 copy-start.5
  0.6 4.2 %shard_map.84 = (bf16[8,208,128]{2,1,0:T(8,128)(2,1)S(1)}, f32[64,128]{1,0:T(8,128)S(1)}) custom-call(f32[1,1024,512]{2,1,0:T(8,128)} %w_ref.1, bf16[2,1,1024,512]{3,2,1,0:T(8,128)(2,1)} %g_ref.1, f32[64,1024]{1,0:T(8,128)} %bitcast.14, f32[64,512]{1,0:T(8,128)} %bitcast.10), custom_call_target="tpu_custom_call" | custom-call | tf_op jit(solution)/shard_map/pallas_call | solution.py:280
  4.8 0.0 copy-start
  4.8 0.0 copy-start.4
  4.8 14.2 %all_to_all.15.in_ref = bf16[8,208,128]{2,1,0:T(8,128)(2,1)S(1)} all-to-all(bf16[8,208,128]{2,1,0:T(8,128)(2,1)S(1)} %get-tuple-element.14), channel_id=1, replica_groups=mesh['gossip_0'=4,'gossip_1'=4,'gossip_2'=2,'mp_0'=2,'mp_1'=4] {'mp_1','..., dimensions={0} | all-to-all | bytes 851968 | tf_op jit(solution)/shard_map/all_to_all | solution.py:298
  19.1 0.0 copy-done.5
  19.1 0.8 %shard_map.85 = bf16[32,2,768]{2,1,0:T(2,128)(2,1)S(1)} custom-call(s32[1,2]{1,0:T(1,128)S(1)} %bitcast.12, bf16[8,208,128]{2,1,0:T(8,128)(2,1)S(1)} %all_to_all.15.in_ref, f32[64,128]{1,0:T(8,128)S(1)} %get-tuple-element.15.own_ref), custom_call_target="tpu_custom_call" | custom-call | tf_op jit(solution)/shard_map/pallas_call | solution.py:299
  19.9 22.1 %all_to_all.16.in_ref = bf16[32,2,768]{2,1,0:T(2,128)(2,1)S(1)} all-to-all(bf16[32,2,768]{2,1,0:T(2,128)(2,1)S(1)} %shard_map.85), channel_id=1, replica_groups=mesh['gossip_0'=4,'gossip_1'=4,'gossip_2'=2,'mp_0'=2,'mp_1'=4] {'gossip_..., dimensions={0} | all-to-all | bytes 196608 | tf_op jit(solution)/shard_map/all_to_all | solution.py:306
  42.0 2.3 %shard_map.86 = (bf16[2,8,16,2,384]{4,3,2,1,0:T(2,128)(2,1)}, f32[16,128]{1,0:T(8,128)S(1)}, f32[2]{0:T(128)}) custom-call(bf16[32,2,768]{2,1,0:T(2,128)(2,1)S(1)} %all_to_all.16.in_ref), custom_call_target="tpu_custom_call" | custom-call | tf_op jit(solution)/shard_map/pallas_call | solution.py:307
  44.3 5.6 %all-to-all-start.2 = ((bf16[256,2,384]{2,1,0:T(2,128)(2,1)}), bf16[256,2,384]{2,1,0:T(2,128)(2,1)S(1)}, u32[]{:S(2)}, u32[]{:S(2)}) async-start(bf16[256,2,384]{2,1,0:T(2,128)(2,1)} %bitcast.4), calls=%async_computation.2 | async-start | bytes 786432 | tf_op jit(solution)/shard_map/all_to_all | solution.py:319
  49.9 0.0 copy-done
  50.0 0.0 copy-done.4
  50.0 0.0 copy-start.1
  50.0 1.6 %copy-done.1 = bf16[2,1,1024,512]{3,2,1,0:T(8,128)(2,1)S(1)} copy-done((bf16[2,1,1024,512]{3,2,1,0:T(8,128)(2,1)S(1)}, bf16[2,1,1024,512]{3,2,1,0:T(8,128)(2,1)}, u32[]{:S(2)}) %copy-start.1) | copy-done | bytes 2097176
  51.6 1.1 %shard_map.87 = (f32[1024,512]{1,0:T(8,128)S(1)}, bf16[2,256,512]{2,1,0:T(8,128)(2,1)S(1)}) custom-call(f32[16,128]{1,0:T(8,128)S(1)} %get-tuple-element.17.vec_ref, f32[1,1024,512]{2,1,0:T(8,128)S(1)} %copy-done, bf16[2,1,1024,512]{3,2,1,0:T(8,128)(2,1)S(1)} %copy-done.1, f32[64,512]{1,0:T(8,128)S(1)} %bitcast.11), custom_call_target="tpu_custom_call" | custom-call | flops 2097152 | bytes 6291456 | tf_op jit(solution)/shard_map/pallas_call | solution.py:320
  52.7 0.0 copy-start.2
  52.7 1.3 %copy-done.2 = f32[1024,512]{1,0:T(8,128)} copy-done((f32[1024,512]{1,0:T(8,128)}, f32[1024,512]{1,0:T(8,128)S(1)}, u32[]{:S(2)}) %copy-start.2) | copy-done | bytes 2097176
  54.0 14.0 %all-to-all-done.2 = bf16[256,2,384]{2,1,0:T(2,128)(2,1)S(1)} async-done(((bf16[256,2,384]{2,1,0:T(2,128)(2,1)}), bf16[256,2,384]{2,1,0:T(2,128)(2,1)S(1)}, u32[]{:S(2)}, u32[]{:S(2)}) %all-to-all-start.2) | async-done | bytes 393248 | tf_op jit(solution)/shard_map/all_to_all | solution.py:319
  67.9 0.1 copy.9
  68.0 0.0 copy-start.3
  68.0 1.6 %copy-done.3 = f32[1024,512]{1,0:T(8,128)S(1)} copy-done((f32[1024,512]{1,0:T(8,128)S(1)}, f32[1024,512]{1,0:T(8,128)}, u32[]{:S(2)}) %copy-start.3) | copy-done | bytes 2097176
  69.6 2.4 %shard_map.88 = (f32[1,1024,512]{2,1,0:T(8,128)}, f32[1,64,1024]{2,1,0:T(8,128)}, f32[2]{0:T(128)}) custom-call(bf16[256,768]{1,0:T(8,128)(2,1)S(1)} %bitcast.9, f32[1024,512]{1,0:T(8,128)S(1)} %copy-done.3, bf16[2,256,512]{2,1,0:T(8,128)(2,1)S(1)} %get-tuple-element.19.right_ref), custom_call_target="tpu_custom_call" | custom-call | tf_op jit(solution)/shard_map/pallas_call | solution.py:340
Async XLA Ops:
  0.6 18.5 %copy-start.5 = (s32[2,1]{0,1:T(1,128)S(1)}, s32[2,1]{0,1:T(1,128)}, u32[]{:S(2)}) copy-start(s32[2,1]{0,1:T(1,128)} %param.9) | copy-start | bytes 28
  4.8 45.1 %copy-start = (f32[1,1024,512]{2,1,0:T(8,128)S(1)}, f32[1,1024,512]{2,1,0:T(8,128)}, u32[]{:S(2)}) copy-start(f32[1,1024,512]{2,1,0:T(8,128)} %w_ref.1) | copy-start | bytes 6291460
  4.8 45.1 %copy-start.4 = (f32[512,64]{0,1:T(8,128)S(1)}, f32[512,64]{0,1:T(8,128)}, u32[]{:S(2)}) copy-start(f32[512,64]{0,1:T(8,128)} %param.8) | copy-start | bytes 393220
  44.3 23.6 %all-to-all-start.2 = ((bf16[256,2,384]{2,1,0:T(2,128)(2,1)}), bf16[256,2,384]{2,1,0:T(2,128)(2,1)S(1)}, u32[]{:S(2)}, u32[]{:S(2)}) async-start(bf16[256,2,384]{2,1,0:T(2,128)(2,1)} %bitcast.4), calls=%async_computation.2 | async-start | bytes 786432 | tf_op jit(solution)/shard_map/all_to_all | solution.py:319
  50.0 1.6 %copy-start.1 = (bf16[2,1,1024,512]{3,2,1,0:T(8,128)(2,1)S(1)}, bf16[2,1,1024,512]{3,2,1,0:T(8,128)(2,1)}, u32[]{:S(2)}) copy-start(bf16[2,1,1024,512]{3,2,1,0:T(8,128)(2,1)} %g_ref.1) | copy-start | bytes 6291460
  52.7 1.3 %copy-start.2 = (f32[1024,512]{1,0:T(8,128)}, f32[1024,512]{1,0:T(8,128)S(1)}, u32[]{:S(2)}) copy-start(f32[1024,512]{1,0:T(8,128)S(1)} %get-tuple-element.18.half_ref) | copy-start | bytes 6291460
  68.0 1.6 %copy-start.3 = (f32[1024,512]{1,0:T(8,128)S(1)}, f32[1024,512]{1,0:T(8,128)}, u32[]{:S(2)}) copy-start(f32[1024,512]{1,0:T(8,128)} %copy-done.2) | copy-start | bytes 6291460

commit v3 on v2

--- a/solution.py
+++ b/solution.py
@@ -18,14 +18,13 @@
 RANK = 64
 SLAB = 4096
 DEVICES = NODES * MP
-SHARE = ROWS // MP
+QUARTER = ROWS // 4
 CHUNKS = 4
 CHUNK = ROWS // CHUNKS
-FIRST = 208
 PARTS = (("w", 0, 512), ("w", 512, 1024), ("g0", 0, 1024), ("g1", 0, 1024))
 MP_ORDER = ("mp_1", "mp_0")
 GOSSIP_ORDER = ("gossip_2", "gossip_0", "gossip_1")
-BACK_ORDER = ("gossip_2", "mp_1", "mp_0", "gossip_0", "gossip_1")
+ALL_ORDER = ("gossip_2", "mp_1", "mp_0", "gossip_0", "gossip_1")
 PLANE = NODES // 2
 TOTAL = NODES * ROWS * SLAB
 
@@ -52,9 +51,10 @@
     return jnp.dot(a, b, preferred_element_type=F32, **kw)
 
 
-def project_kernel(w_hbm, g_hbm, c_hbm, p_hbm, out_ref, own_ref, w, g, c, p, gram, sems):
+def project_kernel(part_hbm, w_hbm, g_hbm, c_hbm, p_hbm, out_ref, part, w, g, c, p, gram, stage, sems):
     me = lax.axis_index(GOSSIP_ORDER)
-    first = pl.multiple_of(lax.axis_index(MP_ORDER) * SHARE, SHARE)
+    col = lax.axis_index(MP_ORDER)
+    first = pl.multiple_of((col // 2) * QUARTER, QUARTER)
     p_copy = pltpu.make_async_copy(p_hbm, p, sems.at[len(PARTS)])
     p_copy.start()
     loads = []
@@ -67,10 +67,12 @@
             copy = pltpu.make_async_copy(g_hbm.at[r, 0, rows], g.at[r, rows], sems.at[i])
         copy.start()
         loads.append(copy)
-    c_copy = pltpu.make_async_copy(c_hbm.at[:, pl.ds(first, SHARE)], c, sems.at[len(PARTS) + 1])
+    c_copy = pltpu.make_async_copy(c_hbm.at[:, pl.ds(first, QUARTER)], c, sems.at[len(PARTS) + 1])
     c_copy.start()
+    part_copy = pltpu.make_async_copy(part_hbm, part, sems.at[len(PARTS) + 2])
+    part_copy.start()
     p_copy.wait()
-    low = lanes((64, 128)) < RANK
+    low = lanes((QUARTER, 128)) < RANK
     pt = p[...]
     hi = rounded(pt)
     lo = rounded(pt - hi)
@@ -81,15 +83,19 @@
     )
     lane = lanes((1, 128))
     row = jnp.where(lane < RANK, gram[pl.ds(me, 1), :], gram[pl.ds(me + NODES, 1), :])
-    row_hi = rounded(row)
+
+    def put(j, x):
+        stage[pl.ds(j, DEVICES, 8), :] = x
+
+    put(6, jnp.broadcast_to(row, (DEVICES, 128)))
     scalars = jnp.zeros((1, 128), F32)
     for (name, begin, end), copy in zip(PARTS, loads):
 
         def store(a, value):
-            for s in range((end - begin) // SHARE):
-                at = s * SHARE
-                packed = jnp.where(low, value[at : at + 64], value[at + 64 : at + 128])
-                out_ref[begin // SHARE + s, 64 * a : 64 * a + 64, :] = packed.astype(BF16)
+            for s in range((end - begin) // 512):
+                at = s * 512
+                packed = jnp.where(low, value[at : at + 256], value[at + 256 : at + 512])
+                put(2 * a + begin // 512 + s, packed)
 
         copy.wait()
         if name == "w":
@@ -105,68 +111,51 @@
             squares = jnp.sum((gf * gf).reshape(ROWS // 8, 8, -1), axis=0)
             total = jnp.sum(squares, axis=(0, 1), keepdims=True)
             hi = rounded(total)
-            scalars = jnp.where(lane == 2 * r, hi, scalars)
-            scalars = jnp.where(lane == 2 * r + 1, total - hi, scalars)
+            scalars = jnp.where(lane == 64 + 2 * r, hi, scalars)
+            scalars = jnp.where(lane == 65 + 2 * r, total - hi, scalars)
     c_copy.wait()
+    part_copy.wait()
+    for r in range(2):
+        mate = part[0, r]
+        place = (mate % 2) * PLANE + mate // 2
+        scalars = jnp.where(lane == 68 + r, place.astype(F32), scalars)
     ct = c[...].T
-    own_ref[...] = jnp.concatenate([ct[:64], ct[64:]], axis=1)
-    at = lax.broadcasted_iota(jnp.int32, (16, 128), 0)
-    extra = jnp.where(at == 0, row_hi, jnp.where(at == 1, row - row_hi, jnp.where(at == 2, scalars, 0.0)))
-    extra = extra.astype(BF16)
-    for m in range(MP):
-        out_ref[m, 192:FIRST, :] = extra
-
-
-def gather_kernel(part_ref, in_ref, own_ref, out_ref):
-    value = in_ref[0].astype(F32)
-    for m in range(1, MP):
-        value += in_ref[m].astype(F32)
-
-    def halves(x):
-        return [x[:32], x[32:]]
-
-    wide = (NODES, 128)
-    row = value[192:193] + value[193:194]
-    row_hi = rounded(row)
-    lane = lanes((1, 128))
-    pair = value[194:195]
-    scalars = jnp.zeros((1, 128), F32)
-    for r in range(2):
-        chosen = (lane == 2 * r) | (lane == 2 * r + 1)
-        total = jnp.sum(jnp.where(chosen, pair, 0.0), axis=1, keepdims=True)
-        hi = rounded(total)
-        scalars = jnp.where(lane == 2 * r, hi, scalars)
-        scalars = jnp.where(lane == 2 * r + 1, total - hi, scalars)
-        mate = part_ref[0, r]
-        place = (mate % 2) * PLANE + mate // 2
-        scalars = jnp.where(lane == 4 + r, place.astype(F32), scalars)
-    upper = halves(value[:64]) + halves(value[64:128])
-    upper += [jnp.broadcast_to(row_hi, wide), jnp.zeros(wide, F32)]
-    lower = halves(value[128:192]) + halves(own_ref[...])
-    lower += [jnp.broadcast_to(row - row_hi, wide), jnp.broadcast_to(scalars, wide)]
-    out_ref[...] = jnp.stack(
-        [jnp.concatenate(upper, axis=1), jnp.concatenate(lower, axis=1)], axis=1
-    ).astype(BF16)
-
-
-def mix_kernel(in_ref, piece_ref, vec_ref, norm_ref):
-    value = in_ref[...].astype(F32)
-    upper, lower = value[:, 0, :], value[:, 1, :]
-    proj, back0 = upper[:, :256], upper[:, 256:512]
-    back1, start = lower[:, :256], lower[:, 256:512]
-    rows = upper[:, 512:640] + lower[:, 512:640]
-    scalars = lower[:, 640:]
+    hi = rounded(ct)
+    own = jnp.where(col % 2 == 0, hi, ct - hi)
+    put(7, jnp.concatenate([own, jnp.zeros_like(own)], axis=1) + scalars)
+    out_ref[...] = stage[...].reshape(DEVICES, 8, 128).astype(BF16)
+
+
+def mix_kernel(in_ref, piece_ref, vec_ref, norm_ref, stage):
+    stage[...] = in_ref[...].astype(F32).reshape(DEVICES * 8, 128)
+
+    def got(m, j):
+        parts = [stage[pl.ds(8 * PLANE * (core * MP + m) + j, PLANE, 8), :] for core in range(2)]
+        return jnp.concatenate(parts, axis=0)
+
+    def summed(j):
+        return functools.reduce(lambda x, y: x + y, [got(m, j) for m in range(MP)])
+
+    proj, back0, back1 = [
+        jnp.concatenate([summed(2 * a), summed(2 * a + 1)], axis=1) for a in range(3)
+    ]
+    rows = summed(6)
+    extras = [got(m, 7) for m in range(MP)]
+    start = jnp.concatenate(
+        [extras[2 * k][:, :RANK] + extras[2 * k + 1][:, :RANK] for k in range(4)], axis=1
+    )
+    scalars = functools.reduce(lambda x, y: x + y, extras)
     lane = lanes((NODES, 128))
     scales = []
     for r in range(2):
-        chosen = (lane == 2 * r) | (lane == 2 * r + 1)
+        chosen = (lane == 64 + 2 * r) | (lane == 65 + 2 * r)
         total = jnp.sum(jnp.where(chosen, scalars, 0.0), axis=(0, 1), keepdims=True)
         norm = jnp.sqrt(total / TOTAL + epsilon)
         scales.append(step_size * jnp.minimum(1.0, clip_limit / norm))
         norm_ref[r] = norm[0, 0]
     pairing = []
     for r in range(2):
-        mate = jnp.sum(jnp.where(lane == 4 + r, scalars, 0.0), axis=1, keepdims=True)
+        mate = jnp.sum(jnp.where(lane == 68 + r, extras[0], 0.0), axis=1, keepdims=True)
         column = lanes((NODES, NODES)).astype(F32)
         pairing.append(jnp.where(column == mate, 1.0, 0.0).astype(BF16))
 
@@ -229,33 +218,22 @@
 
 
 def blend_kernel(in_ref, half_ref, right_ref, out_hbm, pub_ref, cons_ref, out, sems):
-    square = (SHARE, 256)
-    block = lax.broadcasted_iota(jnp.int32, square, 0) // NODES
-    wanted = jnp.where(block == 1, 2, jnp.where(block == 2, 1, block))
-    mine = lanes(square) // RANK == wanted
+    square = (DEVICES, 256)
+    block = lanes(square) // RANK
     zero = jnp.zeros(square, BF16)
-    pick = (lax.broadcasted_iota(jnp.int32, (256, RANK), 0) % RANK == lanes((256, RANK))).astype(F32)
-    pick = pick.astype(BF16)
-
-    def spread(m, begin):
-        rows = [
-            in_ref[(core * MP + m) * PLANE : (core * MP + m + 1) * PLANE, begin : begin + 256]
-            for core in range(2)
-        ]
-        return jnp.where(mine, jnp.concatenate(rows * 4, axis=0), zero)
-
     copies = []
-    per = CHUNK // SHARE
     for k in range(CHUNKS):
-        moved = jnp.concatenate([spread(k * per + s, 0) for s in range(per)], axis=0)
+        moved = jnp.where(block == k, in_ref[:, :256], zero)
         drift = dot(moved, right_ref[0]) + dot(moved, right_ref[1])
         at = pl.ds(k * CHUNK, CHUNK)
         out[at, :] = half_ref[at, :] + mixing * drift
         copy = pltpu.make_async_copy(out.at[at], out_hbm.at[0, at], sems.at[k])
         copy.start()
         copies.append(copy)
+    pick = (lax.broadcasted_iota(jnp.int32, (256, RANK), 0) % RANK == lanes((256, RANK))).astype(F32)
+    pick = pick.astype(BF16)
     for k in range(CHUNKS):
-        sent = jnp.concatenate([spread(k * per + s, 384) for s in range(per)], axis=0)
+        sent = jnp.where(block == k, in_ref[:, 384:640], zero)
         pub_ref[0, :, k * CHUNK : (k + 1) * CHUNK] = lax.dot_general(
             pick, sent, (((0,), (1,)), ((), ())), preferred_element_type=F32
         )
@@ -276,34 +254,28 @@
     hbm = pl.BlockSpec(memory_space=pltpu.HBM)
     limit = pltpu.CompilerParams(vmem_limit_bytes=32 << 20)
     columns = projection.T
-    stay = [pltpu.with_memory_space_constraint(x, pltpu.HBM) for x in (params, gradients, public[0].T, columns)]
-    outgoing, own = pl.pallas_call(
+    pinned = [
+        pltpu.with_memory_space_constraint(x, pltpu.HBM)
+        for x in (partners.T, params, gradients, public[0].T, columns)
+    ]
+    outgoing = pl.pallas_call(
         project_kernel,
-        out_shape=(
-            jax.ShapeDtypeStruct((MP, FIRST, 128), BF16),
-            jax.ShapeDtypeStruct((64, 128), F32),
-        ),
-        in_specs=[hbm, hbm, hbm, hbm],
-        out_specs=(vmem, vmem),
+        out_shape=jax.ShapeDtypeStruct((DEVICES, 8, 128), BF16),
+        in_specs=[hbm] * 5,
+        out_specs=vmem,
         scratch_shapes=[
+            pltpu.SMEM((1, 2), jnp.int32),
             pltpu.VMEM((ROWS, width), F32),
             pltpu.VMEM((2, ROWS, width), BF16),
-            pltpu.VMEM((RANK, SHARE), F32),
+            pltpu.VMEM((RANK, QUARTER), F32),
             pltpu.VMEM((RANK, width), F32),
             pltpu.VMEM((RANK, 128), F32),
-            pltpu.SemaphoreType.DMA((len(PARTS) + 2,)),
+            pltpu.VMEM((DEVICES * 8, 128), F32),
+            pltpu.SemaphoreType.DMA((len(PARTS) + 3,)),
         ],
         compiler_params=limit,
-    )(*stay)
-    arrived = lax.all_to_all(outgoing, MP_ORDER, 0, 0, tiled=True)
-    outgoing = pl.pallas_call(
-        gather_kernel,
-        out_shape=jax.ShapeDtypeStruct((NODES, 2, 768), BF16),
-        in_specs=[smem, vmem, vmem],
-        out_specs=vmem,
-        compiler_params=limit,
-    )(partners.T, arrived, own)
-    arrived = lax.all_to_all(outgoing, GOSSIP_ORDER, 0, 0, tiled=True)
+    )(*pinned)
+    arrived = lax.all_to_all(outgoing, ALL_ORDER, 0, 0, tiled=True)
     piece, scales, norms = pl.pallas_call(
         mix_kernel,
         out_shape=(
@@ -313,10 +285,11 @@
         ),
         in_specs=[vmem],
         out_specs=(vmem, vmem, smem),
+        scratch_shapes=[pltpu.VMEM((DEVICES * 8, 128), F32)],
         compiler_params=limit,
     )(arrived)
     spread = piece.reshape(DEVICES, 2, 384)
-    back = lax.all_to_all(spread, BACK_ORDER, 0, 0, tiled=True).reshape(DEVICES, 768)
+    back = lax.all_to_all(spread, ALL_ORDER, 0, 0, tiled=True).reshape(DEVICES, 768)
     half, right = pl.pallas_call(
         step_kernel,
         grid=(CHUNKS,),
@@ -336,7 +309,7 @@
         ),
         compiler_params=limit,
         cost_estimate=pl.CostEstimate(flops=4 * ROWS * width, bytes_accessed=12 * ROWS * width, transcendentals=0),
-    )(scales, params, gradients, columns)
+    )(scales, pinned[1], pinned[2], columns)
     weights, state, consensus = pl.pallas_call(
         blend_kernel,
         out_shape=(

time: 72.2 us -> 69 us (0.956)
  local copies, waits for them, and re-layouts: 4.55 us -> 0.06 us
  Pallas kernels: 10.7 us -> 12.2 us
  blocking collectives: 36.4 us -> 35.3 us
    unnamed x13 -> x3, local copies, waits for them, and re-layouts: 4.55 us -> 0.06 us
    pallas_call x1, Pallas kernels: 1.08 us -> 3.29 us  [body(): pl.pallas_call(step_kernel, grid=(CHUNKS,), out_shape=(jax.ShapeDtypeStru...]
    all_to_all x2 -> x1, blocking collectives: 36.4 us -> 35.3 us  [body(): arrived = lax.all_to_all(outgoing, ALL_ORDER, 0, 0, tiled=True)]
    pallas_call x2 -> x1, Pallas kernels: 4.95 us -> 4.19 us  [body(): pl.pallas_call(project_kernel, out_shape=jax.ShapeDtypeStruct((DEVICES, 8...]
  transfers between devices with their start and end apart: 1 -> 1, of which waited for: 1 -> 1; matrix products, arithmetic and copies ran while one was open for 0% -> 0% of each run, Pallas kernels for 2% -> 5%
where the time goes in v3:
time: 69 us; the launch traced here: 68.8 us
  blocking collectives  35.3 us (51%)
  waiting for transfers between devices  14.5 us (21%)
  Pallas kernels  12.2 us (18%)
  starting transfers between devices  5.98 us (9%)
    all_to_all x1, blocking collectives, body(): arrived = lax.all_to_all(outgoing, ALL_ORDER, 0, 0, tiled=True)  35.3 us
    all_to_all x1, waiting for transfers between devices, body(): lax.all_to_all(spread, ALL_ORDER, 0, 0, tiled=True).reshape(DEVICES, 768)  14.5 us
    all_to_all x1, starting transfers between devices, body(): lax.all_to_all(spread, ALL_ORDER, 0, 0, tiled=True).reshape(DEVICES, 768)  5.98 us
    pallas_call x1, Pallas kernels, body(): pl.pallas_call(project_kernel, out_shape=jax.ShapeDtypeStruct((DEVICES, 8...  4.19 us
    pallas_call x1, Pallas kernels, body(): pl.pallas_call(step_kernel, grid=(CHUNKS,), out_shape=(jax.ShapeDtypeStru...  3.29 us
    pallas_call x1, Pallas kernels, body(): pl.pallas_call(blend_kernel, out_shape=(jax.ShapeDtypeStruct(params.shape...  2.36 us
    pallas_call x1, Pallas kernels, body(): pl.pallas_call(mix_kernel, out_shape=(jax.ShapeDtypeStruct((2, MP, PLANE,...  2.35 us
  transfers between devices with their start and end apart: 1, of which 1 were waited for; matrix products, arithmetic and copies ran while one was open for 0% of the time, Pallas kernels for 5%

profile of v3, /device:TPU:1, one launch (start us, length us, event | category | flops | bytes accessed | tf_op | source)
XLA Modules:
  0.0 68.8 jit_solution(11823745780854745144)
XLA Ops:
  0.6 4.2 %shard_map.84 = bf16[256,8,128]{2,1,0:T(8,128)(2,1)S(1)} custom-call(s32[1,2]{1,0:T(1,128)} %bitcast.14, f32[1,1024,512]{2,1,0:T(8,128)} %w_ref.1, bf16[2,1,1024,512]{3,2,1,0:T(8,128)(2,1)} %g_ref.1, f32[64,1024]{1,0:T(8,128)} %bitcast.13, f32[64,512]{1,0:T(8,128)} %bitcast.10), custom_call_target="tpu_custom_call" | custom-call | tf_op jit(solution)/shard_map/pallas_call | solution.py:261
  4.8 0.0 copy-start
  4.8 35.3 %all_to_all.10.in_ref = bf16[256,8,128]{2,1,0:T(8,128)(2,1)S(1)} all-to-all(bf16[256,8,128]{2,1,0:T(8,128)(2,1)S(1)} %shard_map.84), channel_id=1, replica_groups=mesh['gossip_0'=4,'gossip_1'=4,'gossip_2'=2,'mp_0'=2,'mp_1'=4] {'gossip_..., dimensions={0} | all-to-all | bytes 1048576 | tf_op jit(solution)/shard_map/all_to_all | solution.py:278
  40.2 2.3 %shard_map.85 = (bf16[2,8,16,2,384]{4,3,2,1,0:T(2,128)(2,1)}, f32[16,128]{1,0:T(8,128)S(1)}, f32[2]{0:T(128)}) custom-call(bf16[256,8,128]{2,1,0:T(8,128)(2,1)S(1)} %all_to_all.10.in_ref), custom_call_target="tpu_custom_call" | custom-call | tf_op jit(solution)/shard_map/pallas_call | solution.py:279
  42.5 6.0 %all-to-all-start.1 = ((bf16[256,2,384]{2,1,0:T(2,128)(2,1)}), bf16[256,2,384]{2,1,0:T(2,128)(2,1)S(1)}, u32[]{:S(2)}, u32[]{:S(2)}) async-start(bf16[256,2,384]{2,1,0:T(2,128)(2,1)} %bitcast.4), calls=%async_computation.1 | async-start | bytes 786432 | tf_op jit(solution)/shard_map/all_to_all | solution.py:292
  48.5 0.0 copy-done
  48.5 3.3 %shard_map.86 = (f32[1024,512]{1,0:T(8,128)S(1)}, bf16[2,256,512]{2,1,0:T(8,128)(2,1)S(1)}) custom-call(f32[16,128]{1,0:T(8,128)S(1)} %get-tuple-element.13.vec_ref, f32[1,1024,512]{2,1,0:T(8,128)} %w_ref.1, bf16[2,1,1024,512]{3,2,1,0:T(8,128)(2,1)} %g_ref.1, f32[64,512]{1,0:T(8,128)S(1)} %bitcast.11), custom_call_target="tpu_custom_call" | custom-call | flops 2097152 | bytes 6291456 | tf_op jit(solution)/shard_map/pallas_call | solution.py:293
  51.8 14.5 %all-to-all-done.1 = bf16[256,2,384]{2,1,0:T(2,128)(2,1)S(1)} async-done(((bf16[256,2,384]{2,1,0:T(2,128)(2,1)}), bf16[256,2,384]{2,1,0:T(2,128)(2,1)S(1)}, u32[]{:S(2)}, u32[]{:S(2)}) %all-to-all-start.1) | async-done | bytes 393248 | tf_op jit(solution)/shard_map/all_to_all | solution.py:292
  66.3 0.1 copy.9
  66.4 2.4 %shard_map.87 = (f32[1,1024,512]{2,1,0:T(8,128)}, f32[1,64,1024]{2,1,0:T(8,128)}, f32[2]{0:T(128)}) custom-call(bf16[256,768]{1,0:T(8,128)(2,1)S(1)} %bitcast.9, f32[1024,512]{1,0:T(8,128)S(1)} %get-tuple-element.14.half_ref, bf16[2,256,512]{2,1,0:T(8,128)(2,1)S(1)} %get-tuple-element.15.right_ref), custom_call_target="tpu_custom_call" | custom-call | tf_op jit(solution)/shard_map/pallas_call | solution.py:313
Async XLA Ops:
  4.8 43.7 %copy-start = (f32[512,64]{0,1:T(8,128)S(1)}, f32[512,64]{0,1:T(8,128)}, u32[]{:S(2)}) copy-start(f32[512,64]{0,1:T(8,128)} %param.8) | copy-start | bytes 393220
  42.5 23.8 %all-to-all-start.1 = ((bf16[256,2,384]{2,1,0:T(2,128)(2,1)}), bf16[256,2,384]{2,1,0:T(2,128)(2,1)S(1)}, u32[]{:S(2)}, u32[]{:S(2)}) async-start(bf16[256,2,384]{2,1,0:T(2,128)(2,1)} %bitcast.4), calls=%async_computation.1 | async-start | bytes 786432 | tf_op jit(solution)/shard_map/all_to_all | solution.py:292

commit v4 on v3

--- a/solution.py
+++ b/solution.py
@@ -21,7 +21,7 @@
 QUARTER = ROWS // 4
 CHUNKS = 4
 CHUNK = ROWS // CHUNKS
-PARTS = (("w", 0, 512), ("w", 512, 1024), ("g0", 0, 1024), ("g1", 0, 1024))
+PARTS = (("g0", 0, 1024), ("g1", 0, 1024), ("w", 0, 512), ("w", 512, 1024))
 MP_ORDER = ("mp_1", "mp_0")
 GOSSIP_ORDER = ("gossip_2", "gossip_0", "gossip_1")
 ALL_ORDER = ("gossip_2", "mp_1", "mp_0", "gossip_0", "gossip_1")
@@ -51,7 +51,7 @@
     return jnp.dot(a, b, preferred_element_type=F32, **kw)
 
 
-def project_kernel(part_hbm, w_hbm, g_hbm, c_hbm, p_hbm, out_ref, part, w, g, c, p, gram, stage, sems):
+def project_kernel(part_hbm, w_hbm, g_hbm, c_hbm, p_hbm, out_ref, part, w, g, c, p, stage, sems):
     me = lax.axis_index(GOSSIP_ORDER)
     col = lax.axis_index(MP_ORDER)
     first = pl.multiple_of((col // 2) * QUARTER, QUARTER)
@@ -77,17 +77,13 @@
     hi = rounded(pt)
     lo = rounded(pt - hi)
     right = jnp.concatenate([hi, hi, lo, lo], axis=0).T.astype(BF16)
-    gram[...] = lax.dot_general(
-        pt, jnp.concatenate([pt, pt], axis=0), (((1,), (1,)), ((), ())),
-        precision=HIGHEST, preferred_element_type=F32,
-    )
+    pair = jnp.concatenate([p[pl.ds(me, 1), :], p[pl.ds(me + NODES, 1), :], jnp.zeros((14, p.shape[1]), F32)], axis=0)
+    pair_hi, pair_lo = split_two(pair)
     lane = lanes((1, 128))
-    row = jnp.where(lane < RANK, gram[pl.ds(me, 1), :], gram[pl.ds(me + NODES, 1), :])
 
     def put(j, x):
         stage[pl.ds(j, DEVICES, 8), :] = x
 
-    put(6, jnp.broadcast_to(row, (DEVICES, 128)))
     scalars = jnp.zeros((1, 128), F32)
     for (name, begin, end), copy in zip(PARTS, loads):
 
@@ -105,7 +101,15 @@
         else:
             r = int(name[1])
             grad = g[r]
-            whole = dot(grad, right)
+            if r == 0:
+                whole = dot(jnp.concatenate([grad, pair_hi, pair_lo], axis=0), right)
+                rows = whole[ROWS:, :128] + whole[ROWS:, 128:]
+                rows = rows[:16] + rows[16:]
+                row = jnp.where(lane < RANK, rows[0:1], rows[1:2])
+                put(6, jnp.broadcast_to(row, (DEVICES, 128)))
+                whole = whole[:ROWS]
+            else:
+                whole = dot(grad, right)
             store(1 + r, whole[:, :128] + whole[:, 128:])
             gf = grad.astype(F32)
             squares = jnp.sum((gf * gf).reshape(ROWS // 8, 8, -1), axis=0)
@@ -126,7 +130,7 @@
     out_ref[...] = stage[...].reshape(DEVICES, 8, 128).astype(BF16)
 
 
-def mix_kernel(in_ref, piece_ref, vec_ref, norm_ref, stage):
+def mix_kernel(in_ref, piece_ref, vec_ref, stage):
     stage[...] = in_ref[...].astype(F32).reshape(DEVICES * 8, 128)
 
     def got(m, j):
@@ -141,18 +145,18 @@
     ]
     rows = summed(6)
     extras = [got(m, 7) for m in range(MP)]
-    start = jnp.concatenate(
-        [extras[2 * k][:, :RANK] + extras[2 * k + 1][:, :RANK] for k in range(4)], axis=1
-    )
+    start_hi, start_lo = [
+        jnp.concatenate([extras[2 * k + n][:, :RANK] for k in range(4)], axis=1) for n in range(2)
+    ]
     scalars = functools.reduce(lambda x, y: x + y, extras)
     lane = lanes((NODES, 128))
-    scales = []
+    scales, norms = [], []
     for r in range(2):
         chosen = (lane == 64 + 2 * r) | (lane == 65 + 2 * r)
         total = jnp.sum(jnp.where(chosen, scalars, 0.0), axis=(0, 1), keepdims=True)
         norm = jnp.sqrt(total / TOTAL + epsilon)
         scales.append(step_size * jnp.minimum(1.0, clip_limit / norm))
-        norm_ref[r] = norm[0, 0]
+        norms.append(norm)
     pairing = []
     for r in range(2):
         mate = jnp.sum(jnp.where(lane == 68 + r, extras[0], 0.0), axis=1, keepdims=True)
@@ -167,23 +171,33 @@
     tall = jnp.concatenate([wide] * 4, axis=0)
     square = (256, 256)
     same = lax.broadcasted_iota(jnp.int32, square, 0) // RANK == lanes(square) // RANK
-    gram = jnp.where(same, tall, 0.0)
-
-    def through(x):
-        return dot(x, gram, precision=HIGHEST)
+    gram_hi, gram_lo = split_two(jnp.where(same, tall, 0.0))
+
+    def through(pairs):
+        upper = jnp.concatenate([x for pair in pairs for x in pair], axis=0)
+        lower = jnp.concatenate([pair[0] for pair in pairs], axis=0)
+        upper, lower = dot(upper, gram_hi), dot(lower, gram_lo)
+        out, at = [], 0
+        for n, pair in enumerate(pairs):
+            total = lower[n * NODES : (n + 1) * NODES]
+            for _ in pair:
+                total += upper[at : at + NODES]
+                at += NODES
+            out.append(total)
+        return out
 
     stepped = proj - scales[0] * back0
-    coef0 = start - through(start) + stepped
+    (moved,) = through([(start_hi.astype(BF16), start_lo.astype(BF16))])
+    coef0 = start_hi + start_lo - moved + stepped
     sent0 = coef0.astype(BF16)
     own0 = sent0.astype(F32)
     drift0 = dot(pairing[0], sent0) - own0
-    both = through(jnp.concatenate([drift0, own0], axis=0))
-    moved0 = both[:NODES]
-    coef1 = own0 - both[NODES:] + (stepped - scales[1] * back1) + mixing * moved0
+    moved0, kept0 = through([split_two(drift0), (sent0,)])
+    coef1 = own0 - kept0 + (stepped - scales[1] * back1) + mixing * moved0
     sent1 = coef1.astype(BF16)
     own1 = sent1.astype(F32)
     drift1 = dot(pairing[1], sent1) - own1
-    moved1 = through(drift1)
+    (moved1,) = through([split_two(drift1)])
     extra = jnp.zeros((NODES, 128), F32)
     for r, (d, moved) in enumerate(((drift0, moved0), (drift1, moved1))):
         total = jnp.sum(d * moved, axis=(0, 1), keepdims=True)
@@ -200,49 +214,56 @@
     for core in range(2):
         for m in range(MP):
             piece_ref[core, m] = piece[core * PLANE : (core + 1) * PLANE]
-    vec_ref[...] = jnp.concatenate(
-        [jnp.broadcast_to(scales[0], (8, 128)), jnp.broadcast_to(scales[1], (8, 128))], axis=0
-    )
-
-
-def step_kernel(vec_ref, w_ref, g_ref, p_ref, out_ref, right_ref):
+    vec_ref[...] = jnp.concatenate([jnp.broadcast_to(x, (8, 128)) for x in scales + norms], axis=0)
+
+
+def step_kernel(vec_ref, w_ref, g_ref, p_ref, out_ref, right_ref, norm_ref):
     scale0 = vec_ref[0:1, 0:1]
     scale1 = vec_ref[8:9, 0:1]
     out_ref[...] = w_ref[0] - scale0 * g_ref[0, 0].astype(F32) - scale1 * g_ref[1, 0].astype(F32)
 
     @pl.when(pl.program_id(0) == 0)
     def _():
-        hi, lo = split_two(p_ref[...])
-        right_ref[0] = jnp.concatenate([hi] * 4, axis=0)
-        right_ref[1] = jnp.concatenate([lo] * 4, axis=0)
-
-
-def blend_kernel(in_ref, half_ref, right_ref, out_hbm, pub_ref, cons_ref, out, sems):
+        for r in range(2):
+            norm_ref[r] = vec_ref[16 + 8 * r, 0]
+        right_ref[...] = jnp.concatenate([p_ref[...].astype(BF16)] * 4, axis=0)
+
+
+def blend_kernel(in_ref, half_ref, right_ref, out_hbm, pub_hbm, cons_hbm, out, pub, cons, sems):
     square = (DEVICES, 256)
     block = lanes(square) // RANK
     zero = jnp.zeros(square, BF16)
     copies = []
-    for k in range(CHUNKS):
-        moved = jnp.where(block == k, in_ref[:, :256], zero)
-        drift = dot(moved, right_ref[0]) + dot(moved, right_ref[1])
-        at = pl.ds(k * CHUNK, CHUNK)
-        out[at, :] = half_ref[at, :] + mixing * drift
-        copy = pltpu.make_async_copy(out.at[at], out_hbm.at[0, at], sems.at[k])
+
+    def send(source, target):
+        copy = pltpu.make_async_copy(source, target, sems.at[len(copies)])
         copy.start()
         copies.append(copy)
-    pick = (lax.broadcasted_iota(jnp.int32, (256, RANK), 0) % RANK == lanes((256, RANK))).astype(F32)
-    pick = pick.astype(BF16)
-    for k in range(CHUNKS):
-        sent = jnp.where(block == k, in_ref[:, 384:640], zero)
-        pub_ref[0, :, k * CHUNK : (k + 1) * CHUNK] = lax.dot_general(
-            pick, sent, (((0,), (1,)), ((), ())), preferred_element_type=F32
-        )
-    extra = in_ref[:, 256:384].astype(F32)
-    lane = lanes((DEVICES, 128))
+
+    def weights(k):
+        moved = jnp.where(block == k, in_ref[:, :256], zero)
+        drift = dot(moved, right_ref[...])
+        for n in range(2):
+            begin = n * CHUNK // 2
+            at = pl.ds(k * CHUNK + begin, CHUNK // 2)
+            out[at, :] = half_ref[at, :] + mixing * drift[begin : begin + CHUNK // 2]
+            send(out.at[at], out_hbm.at[0, at])
+
+    weights(0)
+    weights(1)
+    turned = in_ref[:, 384:640].astype(F32).T
+    for k in range(4):
+        pub[:, k * QUARTER : (k + 1) * QUARTER] = turned[k * RANK : (k + 1) * RANK, :]
+    send(pub, pub_hbm.at[0])
+    weights(2)
+    extra = jnp.sum(in_ref[:, 256:384].astype(F32), axis=0, keepdims=True)
+    lane = lanes((1, 128))
     for r in range(2):
         chosen = (lane == 2 * r) | (lane == 2 * r + 1)
-        total = jnp.sum(jnp.where(chosen, extra, 0.0), axis=(0, 1), keepdims=True)
-        cons_ref[r] = (total / TOTAL)[0, 0]
+        total = jnp.sum(jnp.where(chosen, extra, 0.0), axis=1, keepdims=True)
+        cons[0, r] = (total / TOTAL)[0, 0]
+    send(cons, cons_hbm)
+    weights(3)
     for copy in copies:
         copy.wait()
 
@@ -269,43 +290,43 @@
             pltpu.VMEM((2, ROWS, width), BF16),
             pltpu.VMEM((RANK, QUARTER), F32),
             pltpu.VMEM((RANK, width), F32),
-            pltpu.VMEM((RANK, 128), F32),
             pltpu.VMEM((DEVICES * 8, 128), F32),
             pltpu.SemaphoreType.DMA((len(PARTS) + 3,)),
         ],
         compiler_params=limit,
     )(*pinned)
     arrived = lax.all_to_all(outgoing, ALL_ORDER, 0, 0, tiled=True)
-    piece, scales, norms = pl.pallas_call(
+    piece, scales = pl.pallas_call(
         mix_kernel,
         out_shape=(
             jax.ShapeDtypeStruct((2, MP, PLANE, 2, 384), BF16),
-            jax.ShapeDtypeStruct((16, 128), F32),
-            jax.ShapeDtypeStruct((2,), F32),
+            jax.ShapeDtypeStruct((32, 128), F32),
         ),
         in_specs=[vmem],
-        out_specs=(vmem, vmem, smem),
+        out_specs=(vmem, vmem),
         scratch_shapes=[pltpu.VMEM((DEVICES * 8, 128), F32)],
         compiler_params=limit,
     )(arrived)
     spread = piece.reshape(DEVICES, 2, 384)
     back = lax.all_to_all(spread, ALL_ORDER, 0, 0, tiled=True).reshape(DEVICES, 768)
-    half, right = pl.pallas_call(
+    half, right, norms = pl.pallas_call(
         step_kernel,
         grid=(CHUNKS,),
         out_shape=(
             jax.ShapeDtypeStruct((ROWS, width), F32),
-            jax.ShapeDtypeStruct((2, 256, width), BF16),
+            jax.ShapeDtypeStruct((256, width), BF16),
+            jax.ShapeDtypeStruct((2,), F32),
         ),
         in_specs=[
-            pl.BlockSpec((16, 128), lambda k: (0, 0)),
+            pl.BlockSpec((32, 128), lambda k: (0, 0)),
             pl.BlockSpec((1, CHUNK, width), lambda k: (0, k, 0)),
             pl.BlockSpec((2, 1, CHUNK, width), lambda k: (0, 0, k, 0)),
             pl.BlockSpec((RANK, width), lambda k: (0, 0)),
         ],
         out_specs=(
             pl.BlockSpec((CHUNK, width), lambda k: (k, 0)),
-            pl.BlockSpec((2, 256, width), lambda k: (0, 0, 0)),
+            pl.BlockSpec((256, width), lambda k: (0, 0)),
+            smem,
         ),
         compiler_params=limit,
         cost_estimate=pl.CostEstimate(flops=4 * ROWS * width, bytes_accessed=12 * ROWS * width, transcendentals=0),
@@ -315,14 +336,19 @@
         out_shape=(
             jax.ShapeDtypeStruct(params.shape, F32),
             jax.ShapeDtypeStruct((1, RANK, ROWS), F32),
-            jax.ShapeDtypeStruct((2,), F32),
+            jax.ShapeDtypeStruct((1, 2), F32),
         ),
         in_specs=[vmem, vmem, vmem],
-        out_specs=(hbm, vmem, smem),
-        scratch_shapes=[pltpu.VMEM((ROWS, width), F32), pltpu.SemaphoreType.DMA((CHUNKS,))],
+        out_specs=(hbm, hbm, hbm),
+        scratch_shapes=[
+            pltpu.VMEM((ROWS, width), F32),
+            pltpu.VMEM((RANK, ROWS), F32),
+            pltpu.SMEM((1, 2), F32),
+            pltpu.SemaphoreType.DMA((2 * CHUNKS + 2,)),
+        ],
         compiler_params=limit,
     )(back, half, right)
-    return weights, jnp.swapaxes(state, 1, 2), consensus, norms
+    return weights, jnp.swapaxes(state, 1, 2), consensus[0], norms
 
 
 def solution(mesh):

time: 69 us -> 67.6 us (0.980)
  Pallas kernels: 12.2 us -> 11.4 us
  transfers between devices with their start and end apart: 1 -> 1, of which waited for: 1 -> 1; matrix products, arithmetic and copies ran while one was open for 0% -> 0% of each run, Pallas kernels for 5% -> 6%
where the time goes in v4:
time: 67.6 us; the launch traced here: 67.4 us
  blocking collectives  35.3 us (52%)
  waiting for transfers between devices  14 us (21%)
  Pallas kernels  11.4 us (17%)
  starting transfers between devices  5.97 us (9%)
  between operations  0.68 us (1%)
    all_to_all x1, blocking collectives, body(): arrived = lax.all_to_all(outgoing, ALL_ORDER, 0, 0, tiled=True)  35.3 us
    all_to_all x1, waiting for transfers between devices, body(): lax.all_to_all(spread, ALL_ORDER, 0, 0, tiled=True).reshape(DEVICES, 768)  14 us
    all_to_all x1, starting transfers between devices, body(): lax.all_to_all(spread, ALL_ORDER, 0, 0, tiled=True).reshape(DEVICES, 768)  5.97 us
    pallas_call x1, Pallas kernels, body(): pl.pallas_call(project_kernel, out_shape=jax.ShapeDtypeStruct((DEVICES, 8...  3.88 us
    pallas_call x1, Pallas kernels, body(): pl.pallas_call(step_kernel, grid=(CHUNKS,), out_shape=(jax.ShapeDtypeStru...  3.81 us
    pallas_call x1, Pallas kernels, body(): pl.pallas_call(mix_kernel, out_shape=(jax.ShapeDtypeStruct((2, MP, PLANE,...  1.97 us
    pallas_call x1, Pallas kernels, body(): pl.pallas_call(blend_kernel, out_shape=(jax.ShapeDtypeStruct(params.shape...  1.7 us
  transfers between devices with their start and end apart: 1, of which 1 were waited for; matrix products, arithmetic and copies ran while one was open for 0% of the time, Pallas kernels for 6%

profile of v4, /device:TPU:1, one launch (start us, length us, event | category | flops | bytes accessed | tf_op | source)
XLA Modules:
  0.0 67.4 jit_solution(16521622279007713589)
XLA Ops:
  0.6 3.9 %shard_map.84 = bf16[256,8,128]{2,1,0:T(8,128)(2,1)S(1)} custom-call(s32[1,2]{1,0:T(1,128)} %bitcast.15, f32[1,1024,512]{2,1,0:T(8,128)} %w_ref.1, bf16[2,1,1024,512]{3,2,1,0:T(8,128)(2,1)} %g_ref.1, f32[64,1024]{1,0:T(8,128)} %bitcast.14, f32[64,512]{1,0:T(8,128)} %bitcast.11), custom_call_target="tpu_custom_call" | custom-call | tf_op jit(solution)/shard_map/pallas_call | solution.py:282
  4.5 0.0 copy-start
  4.5 35.3 %all_to_all.10.in_ref = bf16[256,8,128]{2,1,0:T(8,128)(2,1)S(1)} all-to-all(bf16[256,8,128]{2,1,0:T(8,128)(2,1)S(1)} %shard_map.84), channel_id=1, replica_groups=mesh['gossip_0'=4,'gossip_1'=4,'gossip_2'=2,'mp_0'=2,'mp_1'=4] {'gossip_..., dimensions={0} | all-to-all | bytes 1048576 | tf_op jit(solution)/shard_map/all_to_all | solution.py:298
  39.9 2.0 %shard_map.85 = (bf16[2,8,16,2,384]{4,3,2,1,0:T(2,128)(2,1)}, f32[32,128]{1,0:T(8,128)S(1)}) custom-call(bf16[256,8,128]{2,1,0:T(8,128)(2,1)S(1)} %all_to_all.10.in_ref), custom_call_target="tpu_custom_call" | custom-call | tf_op jit(solution)/shard_map/pallas_call | solution.py:299
  41.8 6.0 %all-to-all-start.1 = ((bf16[256,2,384]{2,1,0:T(2,128)(2,1)}), bf16[256,2,384]{2,1,0:T(2,128)(2,1)S(1)}, u32[]{:S(2)}, u32[]{:S(2)}) async-start(bf16[256,2,384]{2,1,0:T(2,128)(2,1)} %bitcast.4), calls=%async_computation.1 | async-start | bytes 786432 | tf_op jit(solution)/shard_map/all_to_all | solution.py:311
  47.8 0.0 copy-done
  47.8 3.8 %shard_map.86 = (f32[1024,512]{1,0:T(8,128)S(1)}, bf16[256,512]{1,0:T(8,128)(2,1)S(1)}, f32[2]{0:T(128)}) custom-call(f32[32,128]{1,0:T(8,128)S(1)} %get-tuple-element.13.vec_ref, f32[1,1024,512]{2,1,0:T(8,128)} %w_ref.1, bf16[2,1,1024,512]{3,2,1,0:T(8,128)(2,1)} %g_ref.1, f32[64,512]{1,0:T(8,128)S(1)} %bitcast.12), custom_call_target="tpu_custom_call" | custom-call | flops 2097152 | bytes 6291456 | tf_op jit(solution)/shard_map/pallas_call | solution.py:312
  51.6 14.0 %all-to-all-done.1 = bf16[256,2,384]{2,1,0:T(2,128)(2,1)S(1)} async-done(((bf16[256,2,384]{2,1,0:T(2,128)(2,1)}), bf16[256,2,384]{2,1,0:T(2,128)(2,1)S(1)}, u32[]{:S(2)}, u32[]{:S(2)}) %all-to-all-start.1) | async-done | bytes 393248 | tf_op jit(solution)/shard_map/all_to_all | solution.py:311
  65.6 0.1 copy.9
  65.7 1.7 %shard_map.87 = (f32[1,1024,512]{2,1,0:T(8,128)}, f32[1,64,1024]{2,1,0:T(8,128)}, f32[1,2]{1,0:T(1,128)}) custom-call(bf16[256,768]{1,0:T(8,128)(2,1)S(1)} %bitcast.10, f32[1024,512]{1,0:T(8,128)S(1)} %get-tuple-element.14.half_ref, bf16[256,512]{1,0:T(8,128)(2,1)S(1)} %get-tuple-element.15.right_ref), custom_call_target="tpu_custom_call" | custom-call | tf_op jit(solution)/shard_map/pallas_call | solution.py:334
Async XLA Ops:
  4.5 43.3 %copy-start = (f32[512,64]{0,1:T(8,128)S(1)}, f32[512,64]{0,1:T(8,128)}, u32[]{:S(2)}) copy-start(f32[512,64]{0,1:T(8,128)} %param.8) | copy-start | bytes 393220
  41.8 23.8 %all-to-all-start.1 = ((bf16[256,2,384]{2,1,0:T(2,128)(2,1)}), bf16[256,2,384]{2,1,0:T(2,128)(2,1)S(1)}, u32[]{:S(2)}, u32[]{:S(2)}) async-start(bf16[256,2,384]{2,1,0:T(2,128)(2,1)} %bitcast.4), calls=%async_computation.1 | async-start | bytes 786432 | tf_op jit(solution)/shard_map/all_to_all | solution.py:311

commit v5 on v4

--- a/solution.py
+++ b/solution.py
@@ -106,6 +106,7 @@
                 rows = whole[ROWS:, :128] + whole[ROWS:, 128:]
                 rows = rows[:16] + rows[16:]
                 row = jnp.where(lane < RANK, rows[0:1], rows[1:2])
+                row = row - jnp.where((lane == me) | (lane == RANK + NODES + me), 1.0 / MP, 0.0)
                 put(6, jnp.broadcast_to(row, (DEVICES, 128)))
                 whole = whole[:ROWS]
             else:
@@ -130,7 +131,7 @@
     out_ref[...] = stage[...].reshape(DEVICES, 8, 128).astype(BF16)
 
 
-def mix_kernel(in_ref, piece_ref, vec_ref, stage):
+def mix_kernel(in_ref, piece_hbm, vec_ref, stage, piece_ref, sems):
     stage[...] = in_ref[...].astype(F32).reshape(DEVICES * 8, 128)
 
     def got(m, j):
@@ -188,16 +189,18 @@
 
     stepped = proj - scales[0] * back0
     (moved,) = through([(start_hi.astype(BF16), start_lo.astype(BF16))])
-    coef0 = start_hi + start_lo - moved + stepped
+    coef0 = stepped - moved
     sent0 = coef0.astype(BF16)
     own0 = sent0.astype(F32)
     drift0 = dot(pairing[0], sent0) - own0
     moved0, kept0 = through([split_two(drift0), (sent0,)])
-    coef1 = own0 - kept0 + (stepped - scales[1] * back1) + mixing * moved0
+    moved0 += drift0
+    coef1 = (stepped - scales[1] * back1) - kept0 + mixing * moved0
     sent1 = coef1.astype(BF16)
     own1 = sent1.astype(F32)
     drift1 = dot(pairing[1], sent1) - own1
     (moved1,) = through([split_two(drift1)])
+    moved1 += drift1
     extra = jnp.zeros((NODES, 128), F32)
     for r, (d, moved) in enumerate(((drift0, moved0), (drift1, moved1))):
         total = jnp.sum(d * moved, axis=(0, 1), keepdims=True)
@@ -211,10 +214,13 @@
         ],
         axis=1,
     ).astype(BF16)
-    for core in range(2):
-        for m in range(MP):
-            piece_ref[core, m] = piece[core * PLANE : (core + 1) * PLANE]
+    piece_ref[...] = piece.reshape(2, PLANE, 2, 384)
+    copies = [pltpu.make_async_copy(piece_ref, piece_hbm.at[:, m], sems.at[m]) for m in range(MP)]
+    for copy in copies:
+        copy.start()
     vec_ref[...] = jnp.concatenate([jnp.broadcast_to(x, (8, 128)) for x in scales + norms], axis=0)
+    for copy in copies:
+        copy.wait()
 
 
 def step_kernel(vec_ref, w_ref, g_ref, p_ref, out_ref, right_ref, norm_ref):
@@ -303,8 +309,12 @@
             jax.ShapeDtypeStruct((32, 128), F32),
         ),
         in_specs=[vmem],
-        out_specs=(vmem, vmem),
-        scratch_shapes=[pltpu.VMEM((DEVICES * 8, 128), F32)],
+        out_specs=(hbm, vmem),
+        scratch_shapes=[
+            pltpu.VMEM((DEVICES * 8, 128), F32),
+            pltpu.VMEM((2, PLANE, 2, 384), BF16),
+            pltpu.SemaphoreType.DMA((MP,)),
+        ],
         compiler_params=limit,
     )(arrived)
     spread = piece.reshape(DEVICES, 2, 384)

time: 67.6 us -> 67.6 us (level)
  no operation moved by 1% of the time
where the time goes in v5:
time: 67.6 us; the launch traced here: 67.3 us
  blocking collectives  35.3 us (52%)
  waiting for transfers between devices  14 us (21%)
  Pallas kernels  11.3 us (17%)
  starting transfers between devices  5.98 us (9%)
  between operations  0.68 us (1%)
    all_to_all x1, blocking collectives, body(): arrived = lax.all_to_all(outgoing, ALL_ORDER, 0, 0, tiled=True)  35.3 us
    all_to_all x1, waiting for transfers between devices, body(): lax.all_to_all(spread, ALL_ORDER, 0, 0, tiled=True).reshape(DEVICES, 768)  14 us
    all_to_all x1, starting transfers between devices, body(): lax.all_to_all(spread, ALL_ORDER, 0, 0, tiled=True).reshape(DEVICES, 768)  5.98 us
    pallas_call x1, Pallas kernels, body(): pl.pallas_call(project_kernel, out_shape=jax.ShapeDtypeStruct((DEVICES, 8...  3.88 us
    pallas_call x1, Pallas kernels, body(): pl.pallas_call(step_kernel, grid=(CHUNKS,), out_shape=(jax.ShapeDtypeStru...  3.81 us
    pallas_call x1, Pallas kernels, body(): pl.pallas_call(mix_kernel, out_shape=(jax.ShapeDtypeStruct((2, MP, PLANE,...  1.91 us
    pallas_call x1, Pallas kernels, body(): pl.pallas_call(blend_kernel, out_shape=(jax.ShapeDtypeStruct(params.shape...  1.7 us
  transfers between devices with their start and end apart: 1, of which 1 were waited for; matrix products, arithmetic and copies ran while one was open for 0% of the time, Pallas kernels for 6%

profile of v5, /device:TPU:1, one launch (start us, length us, event | category | flops | bytes accessed | tf_op | source)
XLA Modules:
  0.0 67.3 jit_solution(13616907803572429311)
XLA Ops:
  0.6 3.9 %shard_map.84 = bf16[256,8,128]{2,1,0:T(8,128)(2,1)S(1)} custom-call(s32[1,2]{1,0:T(1,128)} %bitcast.15, f32[1,1024,512]{2,1,0:T(8,128)} %w_ref.1, bf16[2,1,1024,512]{3,2,1,0:T(8,128)(2,1)} %g_ref.1, f32[64,1024]{1,0:T(8,128)} %bitcast.14, f32[64,512]{1,0:T(8,128)} %bitcast.11), custom_call_target="tpu_custom_call" | custom-call | tf_op jit(solution)/shard_map/pallas_call | solution.py:288
  4.5 0.0 copy-start
  4.5 35.3 %all_to_all.10.in_ref = bf16[256,8,128]{2,1,0:T(8,128)(2,1)S(1)} all-to-all(bf16[256,8,128]{2,1,0:T(8,128)(2,1)S(1)} %shard_map.84), channel_id=1, replica_groups=mesh['gossip_0'=4,'gossip_1'=4,'gossip_2'=2,'mp_0'=2,'mp_1'=4] {'gossip_..., dimensions={0} | all-to-all | bytes 1048576 | tf_op jit(solution)/shard_map/all_to_all | solution.py:304
  39.9 1.9 %shard_map.85 = (bf16[2,8,16,2,384]{4,3,2,1,0:T(2,128)(2,1)}, f32[32,128]{1,0:T(8,128)S(1)}) custom-call(bf16[256,8,128]{2,1,0:T(8,128)(2,1)S(1)} %all_to_all.10.in_ref), custom_call_target="tpu_custom_call" | custom-call | tf_op jit(solution)/shard_map/pallas_call | solution.py:305
  41.8 6.0 %all-to-all-start.1 = ((bf16[256,2,384]{2,1,0:T(2,128)(2,1)}), bf16[256,2,384]{2,1,0:T(2,128)(2,1)S(1)}, u32[]{:S(2)}, u32[]{:S(2)}) async-start(bf16[256,2,384]{2,1,0:T(2,128)(2,1)} %bitcast.4), calls=%async_computation.1 | async-start | bytes 786432 | tf_op jit(solution)/shard_map/all_to_all | solution.py:321
  47.8 0.0 copy-done
  47.8 3.8 %shard_map.86 = (f32[1024,512]{1,0:T(8,128)S(1)}, bf16[256,512]{1,0:T(8,128)(2,1)S(1)}, f32[2]{0:T(128)}) custom-call(f32[32,128]{1,0:T(8,128)S(1)} %get-tuple-element.13.vec_ref, f32[1,1024,512]{2,1,0:T(8,128)} %w_ref.1, bf16[2,1,1024,512]{3,2,1,0:T(8,128)(2,1)} %g_ref.1, f32[64,512]{1,0:T(8,128)S(1)} %bitcast.12), custom_call_target="tpu_custom_call" | custom-call | flops 2097152 | bytes 6291456 | tf_op jit(solution)/shard_map/pallas_call | solution.py:322
  51.6 14.0 %all-to-all-done.1 = bf16[256,2,384]{2,1,0:T(2,128)(2,1)S(1)} async-done(((bf16[256,2,384]{2,1,0:T(2,128)(2,1)}), bf16[256,2,384]{2,1,0:T(2,128)(2,1)S(1)}, u32[]{:S(2)}, u32[]{:S(2)}) %all-to-all-start.1) | async-done | bytes 393248 | tf_op jit(solution)/shard_map/all_to_all | solution.py:321
  65.6 0.1 copy.9
  65.7 1.7 %shard_map.87 = (f32[1,1024,512]{2,1,0:T(8,128)}, f32[1,64,1024]{2,1,0:T(8,128)}, f32[1,2]{1,0:T(1,128)}) custom-call(bf16[256,768]{1,0:T(8,128)(2,1)S(1)} %bitcast.10, f32[1024,512]{1,0:T(8,128)S(1)} %get-tuple-element.14.half_ref, bf16[256,512]{1,0:T(8,128)(2,1)S(1)} %get-tuple-element.15.right_ref), custom_call_target="tpu_custom_call" | custom-call | tf_op jit(solution)/shard_map/pallas_call | solution.py:344
Async XLA Ops:
  4.5 43.2 %copy-start = (f32[512,64]{0,1:T(8,128)S(1)}, f32[512,64]{0,1:T(8,128)}, u32[]{:S(2)}) copy-start(f32[512,64]{0,1:T(8,128)} %param.8) | copy-start | bytes 393220
  41.8 23.8 %all-to-all-start.1 = ((bf16[256,2,384]{2,1,0:T(2,128)(2,1)}), bf16[256,2,384]{2,1,0:T(2,128)(2,1)S(1)}, u32[]{:S(2)}, u32[]{:S(2)}) async-start(bf16[256,2,384]{2,1,0:T(2,128)(2,1)} %bitcast.4), calls=%async_computation.1 | async-start | bytes 786432 | tf_op jit(solution)/shard_map/all_to_all | solution.py:321

commit v6 on v5

--- a/solution.py
+++ b/solution.py
@@ -1,5 +1,3 @@
-import functools
-
 import jax
 import jax.numpy as jnp
 from jax import lax
@@ -131,15 +129,18 @@
     out_ref[...] = stage[...].reshape(DEVICES, 8, 128).astype(BF16)
 
 
-def mix_kernel(in_ref, piece_hbm, vec_ref, stage, piece_ref, sems):
-    stage[...] = in_ref[...].astype(F32).reshape(DEVICES * 8, 128)
+def mix_kernel(in_ref, piece_hbm, vec_ref, stage, sums, piece_ref, sems):
+    value = in_ref[...].astype(F32)
+    stage[...] = value.reshape(DEVICES * 8, 128)
+    value = jnp.sum(value.reshape(2, MP, PLANE, 8, 128), axis=1)
+    sums[...] = value.reshape(NODES * 8, 128)
 
     def got(m, j):
         parts = [stage[pl.ds(8 * PLANE * (core * MP + m) + j, PLANE, 8), :] for core in range(2)]
         return jnp.concatenate(parts, axis=0)
 
     def summed(j):
-        return functools.reduce(lambda x, y: x + y, [got(m, j) for m in range(MP)])
+        return sums[pl.ds(j, NODES, 8), :]
 
     proj, back0, back1 = [
         jnp.concatenate([summed(2 * a), summed(2 * a + 1)], axis=1) for a in range(3)
@@ -149,7 +150,7 @@
     start_hi, start_lo = [
         jnp.concatenate([extras[2 * k + n][:, :RANK] for k in range(4)], axis=1) for n in range(2)
     ]
-    scalars = functools.reduce(lambda x, y: x + y, extras)
+    scalars = summed(7)
     lane = lanes((NODES, 128))
     scales, norms = [], []
     for r in range(2):
@@ -312,6 +313,7 @@
         out_specs=(hbm, vmem),
         scratch_shapes=[
             pltpu.VMEM((DEVICES * 8, 128), F32),
+            pltpu.VMEM((NODES * 8, 128), F32),
             pltpu.VMEM((2, PLANE, 2, 384), BF16),
             pltpu.SemaphoreType.DMA((MP,)),
         ],

time: 67.6 us -> 67.6 us (level)
  no operation moved by 1% of the time
where the time goes in v6:
time: 67.6 us; the launch traced here: 67.4 us
  blocking collectives  35.3 us (52%)
  waiting for transfers between devices  14 us (21%)
  Pallas kernels  11.3 us (17%)
  starting transfers between devices  5.98 us (9%)
  between operations  0.68 us (1%)
    all_to_all x1, blocking collectives, body(): arrived = lax.all_to_all(outgoing, ALL_ORDER, 0, 0, tiled=True)  35.3 us
    all_to_all x1, waiting for transfers between devices, body(): lax.all_to_all(spread, ALL_ORDER, 0, 0, tiled=True).reshape(DEVICES, 768)  14 us
    all_to_all x1, starting transfers between devices, body(): lax.all_to_all(spread, ALL_ORDER, 0, 0, tiled=True).reshape(DEVICES, 768)  5.98 us
    pallas_call x1, Pallas kernels, body(): pl.pallas_call(project_kernel, out_shape=jax.ShapeDtypeStruct((DEVICES, 8...  3.88 us
    pallas_call x1, Pallas kernels, body(): pl.pallas_call(step_kernel, grid=(CHUNKS,), out_shape=(jax.ShapeDtypeStru...  3.81 us
    pallas_call x1, Pallas kernels, body(): pl.pallas_call(mix_kernel, out_shape=(jax.ShapeDtypeStruct((2, MP, PLANE,...  1.93 us
    pallas_call x1, Pallas kernels, body(): pl.pallas_call(blend_kernel, out_shape=(jax.ShapeDtypeStruct(params.shape...  1.69 us
  transfers between devices with their start and end apart: 1, of which 1 were waited for; matrix products, arithmetic and copies ran while one was open for 0% of the time, Pallas kernels for 6%

profile of v6, /device:TPU:1, one launch (start us, length us, event | category | flops | bytes accessed | tf_op | source)
XLA Modules:
  0.0 67.4 jit_solution(2907148102276844837)
XLA Ops:
  0.6 3.9 %shard_map.84 = bf16[256,8,128]{2,1,0:T(8,128)(2,1)S(1)} custom-call(s32[1,2]{1,0:T(1,128)} %bitcast.15, f32[1,1024,512]{2,1,0:T(8,128)} %w_ref.1, bf16[2,1,1024,512]{3,2,1,0:T(8,128)(2,1)} %g_ref.1, f32[64,1024]{1,0:T(8,128)} %bitcast.14, f32[64,512]{1,0:T(8,128)} %bitcast.11), custom_call_target="tpu_custom_call" | custom-call | tf_op jit(solution)/shard_map/pallas_call | solution.py:289
  4.5 0.0 copy-start
  4.5 35.3 %all_to_all.10.in_ref = bf16[256,8,128]{2,1,0:T(8,128)(2,1)S(1)} all-to-all(bf16[256,8,128]{2,1,0:T(8,128)(2,1)S(1)} %shard_map.84), channel_id=1, replica_groups=mesh['gossip_0'=4,'gossip_1'=4,'gossip_2'=2,'mp_0'=2,'mp_1'=4] {'gossip_..., dimensions={0} | all-to-all | bytes 1048576 | tf_op jit(solution)/shard_map/all_to_all | solution.py:305
  39.9 1.9 %shard_map.85 = (bf16[2,8,16,2,384]{4,3,2,1,0:T(2,128)(2,1)}, f32[32,128]{1,0:T(8,128)S(1)}) custom-call(bf16[256,8,128]{2,1,0:T(8,128)(2,1)S(1)} %all_to_all.10.in_ref), custom_call_target="tpu_custom_call" | custom-call | tf_op jit(solution)/shard_map/pallas_call | solution.py:306
  41.8 6.0 %all-to-all-start.1 = ((bf16[256,2,384]{2,1,0:T(2,128)(2,1)}), bf16[256,2,384]{2,1,0:T(2,128)(2,1)S(1)}, u32[]{:S(2)}, u32[]{:S(2)}) async-start(bf16[256,2,384]{2,1,0:T(2,128)(2,1)} %bitcast.4), calls=%async_computation.1 | async-start | bytes 786432 | tf_op jit(solution)/shard_map/all_to_all | solution.py:323
  47.8 0.0 copy-done
  47.8 3.8 %shard_map.86 = (f32[1024,512]{1,0:T(8,128)S(1)}, bf16[256,512]{1,0:T(8,128)(2,1)S(1)}, f32[2]{0:T(128)}) custom-call(f32[32,128]{1,0:T(8,128)S(1)} %get-tuple-element.13.vec_ref, f32[1,1024,512]{2,1,0:T(8,128)} %w_ref.1, bf16[2,1,1024,512]{3,2,1,0:T(8,128)(2,1)} %g_ref.1, f32[64,512]{1,0:T(8,128)S(1)} %bitcast.12), custom_call_target="tpu_custom_call" | custom-call | flops 2097152 | bytes 6291456 | tf_op jit(solution)/shard_map/pallas_call | solution.py:324
  51.6 14.0 %all-to-all-done.1 = bf16[256,2,384]{2,1,0:T(2,128)(2,1)S(1)} async-done(((bf16[256,2,384]{2,1,0:T(2,128)(2,1)}), bf16[256,2,384]{2,1,0:T(2,128)(2,1)S(1)}, u32[]{:S(2)}, u32[]{:S(2)}) %all-to-all-start.1) | async-done | bytes 393248 | tf_op jit(solution)/shard_map/all_to_all | solution.py:323
  65.6 0.1 copy.9
  65.7 1.7 %shard_map.87 = (f32[1,1024,512]{2,1,0:T(8,128)}, f32[1,64,1024]{2,1,0:T(8,128)}, f32[1,2]{1,0:T(1,128)}) custom-call(bf16[256,768]{1,0:T(8,128)(2,1)S(1)} %bitcast.10, f32[1024,512]{1,0:T(8,128)S(1)} %get-tuple-element.14.half_ref, bf16[256,512]{1,0:T(8,128)(2,1)S(1)} %get-tuple-element.15.right_ref), custom_call_target="tpu_custom_call" | custom-call | tf_op jit(solution)/shard_map/pallas_call | solution.py:346
Async XLA Ops:
  4.5 43.3 %copy-start = (f32[512,64]{0,1:T(8,128)S(1)}, f32[512,64]{0,1:T(8,128)}, u32[]{:S(2)}) copy-start(f32[512,64]{0,1:T(8,128)} %param.8) | copy-start | bytes 393220
  41.8 23.8 %all-to-all-start.1 = ((bf16[256,2,384]{2,1,0:T(2,128)(2,1)}), bf16[256,2,384]{2,1,0:T(2,128)(2,1)S(1)}, u32[]{:S(2)}, u32[]{:S(2)}) async-start(bf16[256,2,384]{2,1,0:T(2,128)(2,1)} %bitcast.4), calls=%async_computation.1 | async-start | bytes 786432 | tf_op jit(solution)/shard_map/all_to_all | solution.py:323

commit v7 on v6

--- a/solution.py
+++ b/solution.py
@@ -200,6 +200,20 @@
     sent1 = coef1.astype(BF16)
     own1 = sent1.astype(F32)
     drift1 = dot(pairing[1], sent1) - own1
+    copies = []
+
+    def send(begin, width, upper, lower):
+        part = jnp.stack([upper, lower], axis=1).astype(BF16).reshape(2, PLANE, 2, width)
+        piece_ref[:, :, :, begin : begin + width] = part
+        at = pl.ds(begin, width)
+        for m in range(MP):
+            copy = pltpu.make_async_copy(
+                piece_ref.at[:, :, :, at], piece_hbm.at[:, m, :, :, at], sems.at[len(copies)]
+            )
+            copy.start()
+            copies.append(copy)
+
+    send(0, 256, drift0 + drift1, own1)
     (moved1,) = through([split_two(drift1)])
     moved1 += drift1
     extra = jnp.zeros((NODES, 128), F32)
@@ -208,17 +222,7 @@
         hi = rounded(total)
         extra = jnp.where(lane == 2 * r, hi, extra)
         extra = jnp.where(lane == 2 * r + 1, total - hi, extra)
-    piece = jnp.stack(
-        [
-            jnp.concatenate([drift0 + drift1, extra], axis=1),
-            jnp.concatenate([own1, jnp.zeros((NODES, 128), F32)], axis=1),
-        ],
-        axis=1,
-    ).astype(BF16)
-    piece_ref[...] = piece.reshape(2, PLANE, 2, 384)
-    copies = [pltpu.make_async_copy(piece_ref, piece_hbm.at[:, m], sems.at[m]) for m in range(MP)]
-    for copy in copies:
-        copy.start()
+    send(256, 128, extra, jnp.zeros((NODES, 128), F32))
     vec_ref[...] = jnp.concatenate([jnp.broadcast_to(x, (8, 128)) for x in scales + norms], axis=0)
     for copy in copies:
         copy.wait()
@@ -315,7 +319,7 @@
             pltpu.VMEM((DEVICES * 8, 128), F32),
             pltpu.VMEM((NODES * 8, 128), F32),
             pltpu.VMEM((2, PLANE, 2, 384), BF16),
-            pltpu.SemaphoreType.DMA((MP,)),
+            pltpu.SemaphoreType.DMA((2 * MP,)),
         ],
         compiler_params=limit,
     )(arrived)

time: 67.6 us -> 67.5 us (level)
  no operation moved by 1% of the time
where the time goes in v7:
time: 67.5 us; the launch traced here: 67.3 us
  blocking collectives  35.3 us (52%)
  waiting for transfers between devices  14 us (21%)
  Pallas kernels  11.3 us (17%)
  starting transfers between devices  5.98 us (9%)
  between operations  0.68 us (1%)
    all_to_all x1, blocking collectives, body(): arrived = lax.all_to_all(outgoing, ALL_ORDER, 0, 0, tiled=True)  35.3 us
    all_to_all x1, waiting for transfers between devices, body(): lax.all_to_all(spread, ALL_ORDER, 0, 0, tiled=True).reshape(DEVICES, 768)  14 us
    all_to_all x1, starting transfers between devices, body(): lax.all_to_all(spread, ALL_ORDER, 0, 0, tiled=True).reshape(DEVICES, 768)  5.98 us
    pallas_call x1, Pallas kernels, body(): pl.pallas_call(project_kernel, out_shape=jax.ShapeDtypeStruct((DEVICES, 8...  3.88 us
    pallas_call x1, Pallas kernels, body(): pl.pallas_call(step_kernel, grid=(CHUNKS,), out_shape=(jax.ShapeDtypeStru...  3.81 us
    pallas_call x1, Pallas kernels, body(): pl.pallas_call(mix_kernel, out_shape=(jax.ShapeDtypeStruct((2, MP, PLANE,...  1.87 us
    pallas_call x1, Pallas kernels, body(): pl.pallas_call(blend_kernel, out_shape=(jax.ShapeDtypeStruct(params.shape...  1.7 us
  transfers between devices with their start and end apart: 1, of which 1 were waited for; matrix products, arithmetic and copies ran while one was open for 0% of the time, Pallas kernels for 6%

profile of v7, /device:TPU:1, one launch (start us, length us, event | category | flops | bytes accessed | tf_op | source)
XLA Modules:
  0.0 67.3 jit_solution(11398327382403018658)
XLA Ops:
  0.6 3.9 %shard_map.84 = bf16[256,8,128]{2,1,0:T(8,128)(2,1)S(1)} custom-call(s32[1,2]{1,0:T(1,128)} %bitcast.15, f32[1,1024,512]{2,1,0:T(8,128)} %w_ref.1, bf16[2,1,1024,512]{3,2,1,0:T(8,128)(2,1)} %g_ref.1, f32[64,1024]{1,0:T(8,128)} %bitcast.14, f32[64,512]{1,0:T(8,128)} %bitcast.11), custom_call_target="tpu_custom_call" | custom-call | tf_op jit(solution)/shard_map/pallas_call | solution.py:293
  4.5 0.0 copy-start
  4.5 35.3 %all_to_all.10.in_ref = bf16[256,8,128]{2,1,0:T(8,128)(2,1)S(1)} all-to-all(bf16[256,8,128]{2,1,0:T(8,128)(2,1)S(1)} %shard_map.84), channel_id=1, replica_groups=mesh['gossip_0'=4,'gossip_1'=4,'gossip_2'=2,'mp_0'=2,'mp_1'=4] {'gossip_..., dimensions={0} | all-to-all | bytes 1048576 | tf_op jit(solution)/shard_map/all_to_all | solution.py:309
  39.9 1.9 %shard_map.85 = (bf16[2,8,16,2,384]{4,3,2,1,0:T(2,128)(2,1)}, f32[32,128]{1,0:T(8,128)S(1)}) custom-call(bf16[256,8,128]{2,1,0:T(8,128)(2,1)S(1)} %all_to_all.10.in_ref), custom_call_target="tpu_custom_call" | custom-call | tf_op jit(solution)/shard_map/pallas_call | solution.py:310
  41.7 6.0 %all-to-all-start.1 = ((bf16[256,2,384]{2,1,0:T(2,128)(2,1)}), bf16[256,2,384]{2,1,0:T(2,128)(2,1)S(1)}, u32[]{:S(2)}, u32[]{:S(2)}) async-start(bf16[256,2,384]{2,1,0:T(2,128)(2,1)} %bitcast.4), calls=%async_computation.1 | async-start | bytes 786432 | tf_op jit(solution)/shard_map/all_to_all | solution.py:327
  47.7 0.0 copy-done
  47.7 3.8 %shard_map.86 = (f32[1024,512]{1,0:T(8,128)S(1)}, bf16[256,512]{1,0:T(8,128)(2,1)S(1)}, f32[2]{0:T(128)}) custom-call(f32[32,128]{1,0:T(8,128)S(1)} %get-tuple-element.13.vec_ref, f32[1,1024,512]{2,1,0:T(8,128)} %w_ref.1, bf16[2,1,1024,512]{3,2,1,0:T(8,128)(2,1)} %g_ref.1, f32[64,512]{1,0:T(8,128)S(1)} %bitcast.12), custom_call_target="tpu_custom_call" | custom-call | flops 2097152 | bytes 6291456 | tf_op jit(solution)/shard_map/pallas_call | solution.py:328
  51.6 14.0 %all-to-all-done.1 = bf16[256,2,384]{2,1,0:T(2,128)(2,1)S(1)} async-done(((bf16[256,2,384]{2,1,0:T(2,128)(2,1)}), bf16[256,2,384]{2,1,0:T(2,128)(2,1)S(1)}, u32[]{:S(2)}, u32[]{:S(2)}) %all-to-all-start.1) | async-done | bytes 393248 | tf_op jit(solution)/shard_map/all_to_all | solution.py:327
  65.6 0.1 copy.9
  65.6 1.7 %shard_map.87 = (f32[1,1024,512]{2,1,0:T(8,128)}, f32[1,64,1024]{2,1,0:T(8,128)}, f32[1,2]{1,0:T(1,128)}) custom-call(bf16[256,768]{1,0:T(8,128)(2,1)S(1)} %bitcast.10, f32[1024,512]{1,0:T(8,128)S(1)} %get-tuple-element.14.half_ref, bf16[256,512]{1,0:T(8,128)(2,1)S(1)} %get-tuple-element.15.right_ref), custom_call_target="tpu_custom_call" | custom-call | tf_op jit(solution)/shard_map/pallas_call | solution.py:350
Async XLA Ops:
  4.5 43.2 %copy-start = (f32[512,64]{0,1:T(8,128)S(1)}, f32[512,64]{0,1:T(8,128)}, u32[]{:S(2)}) copy-start(f32[512,64]{0,1:T(8,128)} %param.8) | copy-start | bytes 393220
  41.7 23.8 %all-to-all-start.1 = ((bf16[256,2,384]{2,1,0:T(2,128)(2,1)}), bf16[256,2,384]{2,1,0:T(2,128)(2,1)S(1)}, u32[]{:S(2)}, u32[]{:S(2)}) async-start(bf16[256,2,384]{2,1,0:T(2,128)(2,1)} %bitcast.4), calls=%async_computation.1 | async-start | bytes 786432 | tf_op jit(solution)/shard_map/all_to_all | solution.py:327
